TPU v7x, 32 devices: a whole 2x2x4 slice. The times are simulated.
32 devices in a mesh: lat: 8 (over y, x, core), lon: 4 (over z).
Axes of the slice: x: 2, y: 2, z: 4, core: 2. Of those that a mesh axis runs over, the one named last changes fastest.
Arguments:
- state_field: float32 [96, 96, 256], P('lat', 'lon'), may hold values from -6 to 6
- cotangent: bfloat16 [96, 96, 256], P('lat', 'lon'), may hold values from -6 to 6
- depthwise: float32 [49, 256], replicated, may hold values from -0.875 to 0.875
- norm_gain: float32 [256], replicated, may hold values from 0.4 to 1.6
- w_in: bfloat16 [256, 1024], replicated, may hold values from -0.375 to 0.375
- w_out: bfloat16 [1024, 256], replicated, may hold values from -0.1875 to 0.1875
Outputs:
- block_out: bfloat16 [96, 96, 256], P('lat', 'lon')
- grad_input: bfloat16 [96, 96, 256], P('lat', 'lon')
- weight_grads: float32 [1024, 512], P(('lat', 'lon'))
- grad_depthwise: float32 [49, 256], replicated
- grad_gain: float32 [256], replicated
All inputs are finite; a program needn't handle non-finite values.
Results may differ from a plain program's by a relative error of at most 0.0052.
Values sent between devices are 32-bit elements; how exact they have to be, the bound alone decides.
A program may use at most 64 MiB of HBM per device.

v0:
```python
import math

import jax
import jax.numpy as jnp
from jax import lax
from jax.sharding import PartitionSpec as P


def padded_2(cells, sides, width, closed):
    for axis, dim in sides:
        count = lax.axis_size(axis)
        ends = count if closed else count - 1
        head = lax.slice_in_dim(cells, 0, width, axis=dim)
        tail = lax.slice_in_dim(cells, cells.shape[dim] - width, cells.shape[dim], axis=dim)
        cells = jnp.concatenate(
            [
                lax.ppermute(tail, axis, [(i, (i + 1) % count) for i in range(ends)]),
                cells,
                lax.ppermute(head, axis, [((i + 1) % count, i) for i in range(ends)]),
            ],
            axis=dim,
        )
    return cells


def shifted(value, axis, by):
    peers = lax.axis_size(axis)
    return lax.ppermute(value, axis, [(i, (i + by) % peers) for i in range(peers)])


def gelu_value(values):
    return 0.5 * values * (1.0 + lax.erf(values * 0.7071067811865476))


def gelu_slope(values):
    return (
        0.5 * (1.0 + lax.erf(values * 0.7071067811865476))
        + values * jnp.exp(-0.5 * values * values) * 0.3989422804014327
    )


def layer_norm(convolved, norm_gain):
    average = jnp.mean(convolved, axis=-1, keepdims=True)
    centred_raw = convolved - average
    variance = jnp.mean(centred_raw * centred_raw, axis=-1, keepdims=True)
    inv_std = 1.0 / jnp.sqrt(variance + 1e-06)
    centred = centred_raw * inv_std
    normed = (centred * norm_gain).astype(jnp.bfloat16)
    return (normed, centred, inv_std)


def lat_halo(values):
    return padded_2(values, (("lat", 0),), 3, False)


def lon_halo(values):
    return padded_2(values, (("lon", 1),), 3, True)


def opposite(top_rows, bottom_rows):
    return shifted((top_rows, bottom_rows), "lon", lax.axis_size("lon") // 2)


def widen_rows(values):
    is_first = lax.axis_index("lat") == 0
    is_last = lax.axis_index("lat") == lax.axis_size("lat") - 1
    padded = lat_halo(values)
    top_rows, bottom_rows = opposite(jnp.flip(values[:3], 0), jnp.flip(values[-3:], 0))
    upper_rows = jnp.where(is_first, top_rows, padded[:3])
    lower_rows = jnp.where(is_last, bottom_rows, padded[-3:])
    return jnp.concatenate([upper_rows, padded[3:-3], lower_rows], 0)


def widen_columns(values):
    return lon_halo(values)


def fold_rows(tap_grid):
    is_first = lax.axis_index("lat") == 0
    is_last = lax.axis_index("lat") == lax.axis_size("lat") - 1
    height = tap_grid.shape[0] - 6
    filler = jnp.zeros((height - 6,) + tap_grid.shape[1:], tap_grid.dtype)
    rim_rows = jnp.concatenate([tap_grid[:3], filler, tap_grid[-3:]], 0)
    returned = lat_halo(rim_rows)
    top_rows, bottom_rows = opposite(jnp.flip(tap_grid[:3], 0), jnp.flip(tap_grid[-3:], 0))
    upper_rows = jnp.where(is_first, top_rows, returned[:3])
    lower_rows = jnp.where(is_last, bottom_rows, returned[-3:])
    interior = tap_grid[3:-3]
    return interior.at[:3].add(upper_rows).at[-3:].add(lower_rows)


def fold_columns(tap_grid):
    breadth = tap_grid.shape[1] - 6
    filler = jnp.zeros((tap_grid.shape[0], breadth - 6, tap_grid.shape[2]), tap_grid.dtype)
    rim_cols = jnp.concatenate([tap_grid[:, :3], filler, tap_grid[:, -3:]], 1)
    returned = lon_halo(rim_cols)
    interior = tap_grid[:, 3:-3]
    return interior.at[:, :3].add(returned[:, :3]).at[:, -3:].add(returned[:, -3:])


def apply_taps(extended, depthwise, height, breadth):
    running = jnp.zeros((height, breadth, extended.shape[2]), jnp.float32)
    for row_off in range(7):
        for col_off in range(7):
            running = (
                running
                + depthwise[7 * row_off + col_off]
                * extended[row_off : row_off + height, col_off : col_off + breadth]
            )
    return running


def adjoint_taps(grad_conv, depthwise, height, breadth):
    padded = jnp.pad(grad_conv, ((6, 6), (6, 6), (0, 0)))
    running = jnp.zeros((height + 6, breadth + 6, grad_conv.shape[2]), jnp.float32)
    for row_off in range(7):
        for col_off in range(7):
            running = (
                running
                + depthwise[7 * row_off + col_off]
                * padded[6 - row_off : 12 - row_off + height, 6 - col_off : 12 - col_off + breadth]
            )
    return running


def tap_sums(extended, grad_conv, height, breadth):
    tap_list = []
    for row_off in range(7):
        for col_off in range(7):
            tap_list.append(
                jnp.sum(
                    extended[row_off : row_off + height, col_off : col_off + breadth] * grad_conv,
                    axis=(0, 1),
                )
            )
    return jnp.stack(tap_list, 0)


def body(state_field, cotangent, depthwise, norm_gain, w_in, w_out):
    height, breadth, channels = state_field.shape
    cell_count = height * breadth
    grad_scale = 1.0 / math.sqrt(cell_count * lax.axis_size("lat") * lax.axis_size("lon"))
    extended = widen_columns(widen_rows(state_field))
    convolved = apply_taps(extended, depthwise, height, breadth)
    normed, centred, inv_std = layer_norm(convolved.reshape(cell_count, channels), norm_gain)
    pre_act = jnp.dot(normed, w_in, preferred_element_type=jnp.float32)
    hidden = gelu_value(pre_act).astype(jnp.bfloat16)
    branch = jnp.dot(hidden, w_out, preferred_element_type=jnp.float32)
    block_out = (
        (state_field.reshape(cell_count, channels) + branch)
        .astype(jnp.bfloat16)
        .reshape(height, breadth, channels)
    )
    cot_flat = cotangent.reshape(cell_count, channels)
    grad_hidden = lax.dot_general(
        cot_flat, w_out, (((1,), (1,)), ((), ())), preferred_element_type=jnp.float32
    )
    grad_pre = (grad_hidden * gelu_slope(pre_act)).astype(jnp.bfloat16)
    grad_normed = lax.dot_general(
        grad_pre, w_in, (((1,), (1,)), ((), ())), preferred_element_type=jnp.float32
    )
    scaled_grad = grad_normed * norm_gain
    grad_conv = inv_std * (
        scaled_grad
        - jnp.mean(scaled_grad, axis=-1, keepdims=True)
        - centred * jnp.mean(scaled_grad * centred, axis=-1, keepdims=True)
    )
    gain_local = jnp.sum(grad_normed * centred, axis=0)
    grad_conv = grad_conv.reshape(height, breadth, channels)
    tap_local = tap_sums(extended, grad_conv, height, breadth)
    tap_total, gain_total = lax.psum((tap_local, gain_local), ("lat", "lon"))
    tap_grid = adjoint_taps(grad_conv, depthwise, height, breadth)
    folded = fold_rows(fold_columns(tap_grid))
    grad_input = (cotangent.astype(jnp.float32) + folded).astype(jnp.bfloat16)
    left_part = jnp.einsum("pf,pc->fc", grad_pre, normed, preferred_element_type=jnp.float32)
    right_part = jnp.einsum("pf,pc->fc", hidden, cot_flat, preferred_element_type=jnp.float32)
    weight_grads = lax.psum_scatter(
        jnp.concatenate([left_part, right_part], 1) * grad_scale,
        ("lat", "lon"),
        scatter_dimension=0,
        tiled=True,
    )
    return (block_out, grad_input, weight_grads, tap_total * grad_scale, gain_total * grad_scale)


def solution(mesh):
    placed = (P("lat", "lon", None), P("lat", "lon", None), P(), P(), P(), P())
    return jax.shard_map(
        body,
        mesh=mesh,
        in_specs=placed,
        out_specs=(P("lat", "lon", None), P("lat", "lon", None), P(("lat", "lon"), None), P(), P()),
        check_vma=False,
    )
```

profile of v0, /device:TPU:0, one launch (start us, length us, event | category | flops | bytes accessed | tf_op | source)
XLA Modules:
  0.0 189.4 jit_solution(11335253484696414345)
XLA Ops:
  7.2 1.0 fusion.115
  8.3 2.4 %collective-permute-start.1 = (f32[3,24,256]{2,1,0:T(8,128)S(1)}, f32[3,24,256]{2,1,0:T(8,128)S(1)}, u32[]{:S(2)}, u32[]{:S(2)}) collective-permute-start(f32[3,24,256]{2,1,0:T(8,128)S(1)} %get-tuple-element.134), channel_id=1, source_target_pairs={{0,4},{4,8},{8,12},{12,16},{16,20},{20,24},{24,28},{1,5},{5,9},{9,... | collective-permute-start | bytes 221192 | tf_op jit(solution)/shard_map/ppermute | solution.py:17
  10.6 3.5 %collective-permute-start.2 = (f32[3,24,256]{2,1,0:T(8,128)S(1)}, f32[3,24,256]{2,1,0:T(8,128)S(1)}, u32[]{:S(2)}, u32[]{:S(2)}) collective-permute-start(f32[3,24,256]{2,1,0:T(8,128)S(1)} %rev.14), channel_id=1, source_target_pairs={{0,2},{1,3},{2,0},{3,1},{4,6},{5,7},{6,4},{7,5},{8,10},{9,11},{10,... | collective-permute-start | bytes 221192 | tf_op jit(solution)/shard_map/ppermute | solution.py:28
  14.1 1.3 collective-permute-start.3
  15.5 1.0 fusion.116
  16.6 1.0 fusion.117
  17.8 0.4 collective-permute-done.3
  18.3 2.5 %collective-permute-done = f32[3,24,256]{2,1,0:T(8,128)S(1)} collective-permute-done((f32[3,24,256]{2,1,0:T(8,128)S(1)}, f32[3,24,256]{2,1,0:T(8,128)S(1)}, u32[]{:S(2)}, u32[]{:S(2)}) %collective-permute-start) | collective-permute-done | bytes 73760 | tf_op jit(solution)/shard_map/ppermute | solution.py:28
  20.8 2.2 %collective-permute-start.4 = (f32[18,3,256]{2,1,0:T(4,128)S(1)}, f32[18,3,256]{2,1,0:T(4,128)S(1)}, u32[]{:S(2)}, u32[]{:S(2)}) collective-permute-start(f32[18,3,256]{2,1,0:T(4,128)S(1)} %get-tuple-element.131), channel_id=1, source_target_pairs={{0,1},{1,2},{2,3},{3,0},{4,5},{5,6},{6,7},{7,4},{8,9},{9,10},{10,1... | collective-permute-start | bytes 165896 | tf_op jit(solution)/shard_map/ppermute | solution.py:17
  23.0 2.9 %collective-permute-start.5 = (f32[18,3,256]{2,1,0:T(4,128)S(1)}, f32[18,3,256]{2,1,0:T(4,128)S(1)}, u32[]{:S(2)}, u32[]{:S(2)}) collective-permute-start(f32[18,3,256]{2,1,0:T(4,128)S(1)} %get-tuple-element.132), channel_id=1, source_target_pairs={{1,0},{2,1},{3,2},{0,3},{5,4},{6,5},{7,6},{4,7},{9,8},{10,9},{11,1... | collective-permute-start | bytes 165896 | tf_op jit(solution)/shard_map/ppermute | solution.py:19
  25.9 0.9 fusion.118
  27.0 1.9 collective-permute-done.4
  29.1 2.3 %fusion.112 = (f32[12,24]{1,0:T(8,128)S(1)}, f32[12,24,256]{2,1,0:T(8,128)S(1)}) fusion(f32[18,27,256]{2,1,0:T(8,128)S(1)} %get-tuple-element.130, f32[256]{0:T(256)S(1)} %bitcast.222, f32[256]{0:T(256)S(1)} %bitcast.224, f32[256]{0:T(256)S(1)} %bitcast.130, f32[3,24,256]{2,1,0:T(8,128)S(1)} %broadcast_select_fusion, f32[12,24,256]{2,1,0:T(8,128)S(1)} %copy-done.1, ...), kind=kLoop, calls=%fused_computation.252 | loop fusion | flops 7667424 | bytes 13174912 | tf_op jit(solution)/shard_map/reduce_sum | solution.py:43
  32.2 0.4 multiply_convert_fusion
  32.6 0.5 copy-done.2
  33.1 0.2 copy-done.3
  33.3 0.6 fusion
  33.9 1.1 multiply_reduce_fusion
  35.0 0.5 fusion.110
  35.5 0.5 fusion.119
  36.0 1.5 maximum_multiply_fusion
  37.5 2.9 %copy.13 = f32[1024,512]{1,0:T(8,128)} copy(f32[1024,512]{0,1:T(8,128)} %maximum_multiply_fusion) | data formatting | bytes 4194304
  40.4 0.7 broadcast_multiply_fusion.2
  41.2 0.2 subtract_multiply_fusion
  41.4 4.3 %fusion.99 = f32[18,30,256]{2,1,0:T(8,128)S(1)} fusion(f32[12,24,256]{2,1,0:T(8,128)S(1)} %bitcast.119, f32[256]{0:T(256)} %bitcast.223, f32[256]{0:T(256)} %bitcast.225, f32[256]{0:T(256)S(1)} %bitcast.131, f32[256]{0:T(256)S(1)} %bitcast.133, f32[256]{0:T(256)S(1)} %bitcast.135, f32[256]{0:T(256)S(1)} %bitcast.137, f32[256]{0:T(256)S(1)} %bitcast.139, ...), kind=kLoop, calls=%fused_computation.154 | loop fusion | flops 13409280 | bytes 898048 | tf_op jit(solution)/shard_map/add | solution.py:119
  45.7 0.7 fusion.113
  46.4 2.0 %collective-permute-start.6 = (f32[18,3,256]{2,1,0:T(4,128)}, f32[18,3,256]{2,1,0:T(4,128)S(1)}, u32[]{:S(2)}, u32[]{:S(2)}) collective-permute-start(f32[18,3,256]{2,1,0:T(4,128)} %get-tuple-element.126), channel_id=1, source_target_pairs={{0,1},{1,2},{2,3},{3,0},{4,5},{5,6},{6,7},{7,4},{8,9},{9,10},{10,1... | collective-permute-start | bytes 165896 | tf_op jit(solution)/shard_map/ppermute | solution.py:17
  48.4 0.7 multiply_reduce_fusion.47
  49.1 0.9 multiply_reduce_fusion.4
  50.0 0.5 multiply_reduce_fusion.5
  50.5 1.1 multiply_reduce_fusion.1
  51.7 2.2 %stack.199 = f32[49,256]{1,0:T(8,128)S(1)} concatenate(f32[1,256]{1,0:T(1,128)} %bitcast.274, f32[1,256]{1,0:T(1,128)} %bitcast.273, f32[1,256]{1,0:T(1,128)} %bitcast.272, f32[1,256]{1,0:T(1,128)S(1)} %bitcast.230, f32[1,256]{1,0:T(1,128)S(1)} %bitcast.233, f32[1,256]{1,0:T(1,128)S(1)} %bitcast.234, f32[1,256]{1,0:T(1,128)S(1)} %bitcast.235, f32[1,256]{1,0:T(1,128)S(1)} %bitcast.253, ...), dimensions={0} | concatenate | bytes 100352 | tf_op jit(solution)/shard_map/stack | solution.py:136
  53.9 41.8 %all-reduce.1 = (f32[49,256]{1,0:T(8,128)S(1)}, f32[256]{0:T(256)S(1)}) all-reduce(f32[49,256]{1,0:T(8,128)S(1)} %stack.199, f32[256]{0:T(256)} %get-tuple-element.111), channel_id=1, replica_groups=mesh['lat'=8,'lon'=4] {'lat','lon'}, use_global_device_ids=true, to_apply=%region_54.55 | all-reduce | flops 12800 | bytes 102400 | tf_op jit(solution)/shard_map/psum | solution.py:171
  95.7 1.0 fusion.5
  96.7 0.6 broadcast_multiply_fusion
  97.4 2.4 %collective-permute-start.7 = (f32[18,3,256]{2,1,0:T(4,128)S(1)}, f32[18,3,256]{2,1,0:T(4,128)S(1)}, u32[]{:S(2)}, u32[]{:S(2)}) collective-permute-start(f32[18,3,256]{2,1,0:T(4,128)S(1)} %copy-done.5), channel_id=1, source_target_pairs={{1,0},{2,1},{3,2},{0,3},{5,4},{6,5},{7,6},{4,7},{9,8},{10,9},{11,1... | collective-permute-start | bytes 165896 | tf_op jit(solution)/shard_map/ppermute | solution.py:19
  99.9 0.3 scatter-add.14
  100.1 2.4 %collective-permute-done.7 = f32[18,3,256]{2,1,0:T(4,128)S(1)} collective-permute-done((f32[18,3,256]{2,1,0:T(4,128)S(1)}, f32[18,3,256]{2,1,0:T(4,128)S(1)}, u32[]{:S(2)}, u32[]{:S(2)}) %collective-permute-start.7) | collective-permute-done | bytes 55328 | tf_op jit(solution)/shard_map/ppermute | solution.py:19
  102.5 0.2 scatter-add.15
  102.8 1.6 collective-permute-start.8
  104.4 1.3 collective-permute-start.9
  105.7 0.6 broadcast_multiply_fusion.4
  106.3 1.3 collective-permute-start.11
  107.6 1.4 collective-permute-start.10
  109.0 1.8 collective-permute-done.8
  110.9 2.1 %collective-permute-done.10 = f32[3,24,256]{2,1,0:T(8,128)S(1)} collective-permute-done((f32[3,24,256]{2,1,0:T(8,128)S(1)}, f32[3,24,256]{2,1,0:T(8,128)S(1)}, u32[]{:S(2)}, u32[]{:S(2)}) %collective-permute-start.10) | collective-permute-done | bytes 73760 | tf_op jit(solution)/shard_map/ppermute | solution.py:28
  113.0 0.7 add_convert_fusion
  113.7 68.9 %reduce-scatter.4.cloned.1.call-done = f32[32,512]{1,0:T(8,128)} async-done(((f32[1024,512]{1,0:T(8,128)}), f32[32,512]{1,0:T(8,128)}) %reduce-scatter.4.cloned.1.call-update) | async-done | bytes 65552
  (122 shorter events, 1.3 us)
Async XLA Ops:
  7.2 25.0 %copy-start = (bf16[256,1024]{1,0:T(8,128)(2,1)S(1)}, bf16[256,1024]{1,0:T(8,128)(2,1)}, u32[]{:S(2)}) copy-start(bf16[256,1024]{1,0:T(8,128)(2,1)} %param.18) | copy-start | bytes 1572868
  7.2 13.6 %copy-start.1 = (f32[12,24,256]{2,1,0:T(8,128)S(1)}, f32[12,24,256]{2,1,0:T(8,128)}, u32[]{:S(2)}) copy-start(f32[12,24,256]{2,1,0:T(8,128)} %param.14) | copy-start | bytes 884740
  7.2 175.4 %reduce-scatter.4.cloned.1.call-start = ((), (), s32[]{:S(2)}) async-start(), calls=%async_computation.1 | async-start | bytes 2162688
  8.3 12.5 %collective-permute-start.1 = (f32[3,24,256]{2,1,0:T(8,128)S(1)}, f32[3,24,256]{2,1,0:T(8,128)S(1)}, u32[]{:S(2)}, u32[]{:S(2)}) collective-permute-start(f32[3,24,256]{2,1,0:T(8,128)S(1)} %get-tuple-element.134), channel_id=1, source_target_pairs={{0,4},{4,8},{8,12},{12,16},{16,20},{20,24},{24,28},{1,5},{5,9},{9,... | collective-permute-start | bytes 221192 | tf_op jit(solution)/shard_map/ppermute | solution.py:17
  10.6 7.2 %collective-permute-start.2 = (f32[3,24,256]{2,1,0:T(8,128)S(1)}, f32[3,24,256]{2,1,0:T(8,128)S(1)}, u32[]{:S(2)}, u32[]{:S(2)}) collective-permute-start(f32[3,24,256]{2,1,0:T(8,128)S(1)} %rev.14), channel_id=1, source_target_pairs={{0,2},{1,3},{2,0},{3,1},{4,6},{5,7},{6,4},{7,5},{8,10},{9,11},{10,... | collective-permute-start | bytes 221192 | tf_op jit(solution)/shard_map/ppermute | solution.py:28
  14.1 4.1 %collective-permute-start.3 = (f32[3,24,256]{2,1,0:T(8,128)S(1)}, f32[3,24,256]{2,1,0:T(8,128)S(1)}, u32[]{:S(2)}, u32[]{:S(2)}) collective-permute-start(f32[3,24,256]{2,1,0:T(8,128)S(1)} %get-tuple-element.133), channel_id=1, source_target_pairs={{4,0},{8,4},{12,8},{16,12},{20,16},{24,20},{28,24},{5,1},{9,5},{13... | collective-permute-start | bytes 221192 | tf_op jit(solution)/shard_map/ppermute | solution.py:19
  15.4 5.3 %collective-permute-start = (f32[3,24,256]{2,1,0:T(8,128)S(1)}, f32[3,24,256]{2,1,0:T(8,128)S(1)}, u32[]{:S(2)}, u32[]{:S(2)}) collective-permute-start(f32[3,24,256]{2,1,0:T(8,128)S(1)} %rev.13), channel_id=1, source_target_pairs={{0,2},{1,3},{2,0},{3,1},{4,6},{5,7},{6,4},{7,5},{8,10},{9,11},{10,... | collective-permute-start | bytes 221192 | tf_op jit(solution)/shard_map/ppermute | solution.py:28
  16.6 14.9 %copy-start.7 = (f32[1,256]{1,0:T(1,128)}, f32[1,256]{1,0:T(1,128)S(1)}, u32[]{:S(2)}) copy-start(f32[1,256]{1,0:T(1,128)S(1)} %get-tuple-element.152) | copy-start | bytes 3076
  16.6 14.9 %copy-start.8 = (f32[1,256]{1,0:T(1,128)}, f32[1,256]{1,0:T(1,128)S(1)}, u32[]{:S(2)}) copy-start(f32[1,256]{1,0:T(1,128)S(1)} %get-tuple-element.153) | copy-start | bytes 3076
  17.6 11.3 %copy-start.10 = (f32[1,256]{1,0:T(1,128)}, f32[1,256]{1,0:T(1,128)S(1)}, u32[]{:S(2)}) copy-start(f32[1,256]{1,0:T(1,128)S(1)} %get-tuple-element.155) | copy-start | bytes 3076
  17.6 11.3 %copy-start.11 = (f32[1,256]{1,0:T(1,128)}, f32[1,256]{1,0:T(1,128)S(1)}, u32[]{:S(2)}) copy-start(f32[1,256]{1,0:T(1,128)S(1)} %get-tuple-element.156) | copy-start | bytes 3076
  17.6 11.3 %copy-start.12 = (f32[1,256]{1,0:T(1,128)}, f32[1,256]{1,0:T(1,128)S(1)}, u32[]{:S(2)}) copy-start(f32[1,256]{1,0:T(1,128)S(1)} %get-tuple-element.157) | copy-start | bytes 3076
  17.6 11.3 %copy-start.13 = (f32[1,256]{1,0:T(1,128)}, f32[1,256]{1,0:T(1,128)S(1)}, u32[]{:S(2)}) copy-start(f32[1,256]{1,0:T(1,128)S(1)} %get-tuple-element.158) | copy-start | bytes 3076
  17.6 11.3 %copy-start.14 = (f32[1,256]{1,0:T(1,128)}, f32[1,256]{1,0:T(1,128)S(1)}, u32[]{:S(2)}) copy-start(f32[1,256]{1,0:T(1,128)S(1)} %get-tuple-element.159) | copy-start | bytes 3076
  17.7 11.3 %copy-start.15 = (f32[1,256]{1,0:T(1,128)}, f32[1,256]{1,0:T(1,128)S(1)}, u32[]{:S(2)}) copy-start(f32[1,256]{1,0:T(1,128)S(1)} %get-tuple-element.160) | copy-start | bytes 3076
  17.7 11.3 %copy-start.16 = (f32[1,256]{1,0:T(1,128)}, f32[1,256]{1,0:T(1,128)S(1)}, u32[]{:S(2)}) copy-start(f32[1,256]{1,0:T(1,128)S(1)} %get-tuple-element.161) | copy-start | bytes 3076
  17.7 11.3 %copy-start.17 = (f32[1,256]{1,0:T(1,128)}, f32[1,256]{1,0:T(1,128)S(1)}, u32[]{:S(2)}) copy-start(f32[1,256]{1,0:T(1,128)S(1)} %get-tuple-element.162) | copy-start | bytes 3076
  17.7 11.3 %copy-start.18 = (f32[1,256]{1,0:T(1,128)}, f32[1,256]{1,0:T(1,128)S(1)}, u32[]{:S(2)}) copy-start(f32[1,256]{1,0:T(1,128)S(1)} %get-tuple-element.163) | copy-start | bytes 3076
  17.7 11.3 %copy-start.19 = (f32[1,256]{1,0:T(1,128)}, f32[1,256]{1,0:T(1,128)S(1)}, u32[]{:S(2)}) copy-start(f32[1,256]{1,0:T(1,128)S(1)} %get-tuple-element.164) | copy-start | bytes 3076
  17.7 11.3 %copy-start.20 = (f32[1,256]{1,0:T(1,128)}, f32[1,256]{1,0:T(1,128)S(1)}, u32[]{:S(2)}) copy-start(f32[1,256]{1,0:T(1,128)S(1)} %get-tuple-element.165) | copy-start | bytes 3076
  17.7 11.3 %copy-start.21 = (f32[1,256]{1,0:T(1,128)}, f32[1,256]{1,0:T(1,128)S(1)}, u32[]{:S(2)}) copy-start(f32[1,256]{1,0:T(1,128)S(1)} %get-tuple-element.166) | copy-start | bytes 3076
  17.7 11.3 %copy-start.22 = (f32[1,256]{1,0:T(1,128)}, f32[1,256]{1,0:T(1,128)S(1)}, u32[]{:S(2)}) copy-start(f32[1,256]{1,0:T(1,128)S(1)} %get-tuple-element.167) | copy-start | bytes 3076
  17.7 11.3 %copy-start.23 = (f32[1,256]{1,0:T(1,128)}, f32[1,256]{1,0:T(1,128)S(1)}, u32[]{:S(2)}) copy-start(f32[1,256]{1,0:T(1,128)S(1)} %get-tuple-element.168) | copy-start | bytes 3076
  17.7 11.3 %copy-start.24 = (f32[1,256]{1,0:T(1,128)}, f32[1,256]{1,0:T(1,128)S(1)}, u32[]{:S(2)}) copy-start(f32[1,256]{1,0:T(1,128)S(1)} %get-tuple-element.169) | copy-start | bytes 3076
  17.8 11.3 %copy-start.25 = (f32[1,256]{1,0:T(1,128)}, f32[1,256]{1,0:T(1,128)S(1)}, u32[]{:S(2)}) copy-start(f32[1,256]{1,0:T(1,128)S(1)} %get-tuple-element.170) | copy-start | bytes 3076
  17.8 11.3 %copy-start.26 = (f32[1,256]{1,0:T(1,128)}, f32[1,256]{1,0:T(1,128)S(1)}, u32[]{:S(2)}) copy-start(f32[1,256]{1,0:T(1,128)S(1)} %get-tuple-element.171) | copy-start | bytes 3076
  17.8 11.3 %copy-start.27 = (f32[1,256]{1,0:T(1,128)}, f32[1,256]{1,0:T(1,128)S(1)}, u32[]{:S(2)}) copy-start(f32[1,256]{1,0:T(1,128)S(1)} %get-tuple-element.172) | copy-start | bytes 3076
  17.8 13.7 %copy-start.9 = (f32[1,256]{1,0:T(1,128)}, f32[1,256]{1,0:T(1,128)S(1)}, u32[]{:S(2)}) copy-start(f32[1,256]{1,0:T(1,128)S(1)} %get-tuple-element.154) | copy-start | bytes 3076
  20.8 8.0 %collective-permute-start.4 = (f32[18,3,256]{2,1,0:T(4,128)S(1)}, f32[18,3,256]{2,1,0:T(4,128)S(1)}, u32[]{:S(2)}, u32[]{:S(2)}) collective-permute-start(f32[18,3,256]{2,1,0:T(4,128)S(1)} %get-tuple-element.131), channel_id=1, source_target_pairs={{0,1},{1,2},{2,3},{3,0},{4,5},{5,6},{6,7},{7,4},{8,9},{9,10},{10,1... | collective-permute-start | bytes 165896 | tf_op jit(solution)/shard_map/ppermute | solution.py:17
  23.0 5.8 %collective-permute-start.5 = (f32[18,3,256]{2,1,0:T(4,128)S(1)}, f32[18,3,256]{2,1,0:T(4,128)S(1)}, u32[]{:S(2)}, u32[]{:S(2)}) collective-permute-start(f32[18,3,256]{2,1,0:T(4,128)S(1)} %get-tuple-element.132), channel_id=1, source_target_pairs={{1,0},{2,1},{3,2},{0,3},{5,4},{6,5},{7,6},{4,7},{9,8},{10,9},{11,1... | collective-permute-start | bytes 165896 | tf_op jit(solution)/shard_map/ppermute | solution.py:19
  26.8 4.6 %copy-start.28 = (f32[1,256]{1,0:T(1,128)}, f32[1,256]{1,0:T(1,128)S(1)}, u32[]{:S(2)}) copy-start(f32[1,256]{1,0:T(1,128)S(1)} %get-tuple-element.173) | copy-start | bytes 3076
  26.9 4.6 %copy-start.29 = (f32[1,256]{1,0:T(1,128)}, f32[1,256]{1,0:T(1,128)S(1)}, u32[]{:S(2)}) copy-start(f32[1,256]{1,0:T(1,128)S(1)} %get-tuple-element.174) | copy-start | bytes 3076
  26.9 4.6 %copy-start.30 = (f32[1,256]{1,0:T(1,128)}, f32[1,256]{1,0:T(1,128)S(1)}, u32[]{:S(2)}) copy-start(f32[1,256]{1,0:T(1,128)S(1)} %get-tuple-element.175) | copy-start | bytes 3076
  26.9 4.6 %copy-start.31 = (f32[1,256]{1,0:T(1,128)}, f32[1,256]{1,0:T(1,128)S(1)}, u32[]{:S(2)}) copy-start(f32[1,256]{1,0:T(1,128)S(1)} %get-tuple-element.176) | copy-start | bytes 3076
  26.9 4.6 %copy-start.32 = (f32[1,256]{1,0:T(1,128)}, f32[1,256]{1,0:T(1,128)S(1)}, u32[]{:S(2)}) copy-start(f32[1,256]{1,0:T(1,128)S(1)} %get-tuple-element.177) | copy-start | bytes 3076
  26.9 4.6 %copy-start.33 = (f32[1,256]{1,0:T(1,128)}, f32[1,256]{1,0:T(1,128)S(1)}, u32[]{:S(2)}) copy-start(f32[1,256]{1,0:T(1,128)S(1)} %get-tuple-element.178) | copy-start | bytes 3076
  26.9 4.6 %copy-start.34 = (f32[1,256]{1,0:T(1,128)}, f32[1,256]{1,0:T(1,128)S(1)}, u32[]{:S(2)}) copy-start(f32[1,256]{1,0:T(1,128)S(1)} %get-tuple-element.179) | copy-start | bytes 3076
  26.9 4.6 %copy-start.35 = (f32[1,256]{1,0:T(1,128)}, f32[1,256]{1,0:T(1,128)S(1)}, u32[]{:S(2)}) copy-start(f32[1,256]{1,0:T(1,128)S(1)} %get-tuple-element.180) | copy-start | bytes 3076
  26.9 4.6 %copy-start.36 = (f32[1,256]{1,0:T(1,128)}, f32[1,256]{1,0:T(1,128)S(1)}, u32[]{:S(2)}) copy-start(f32[1,256]{1,0:T(1,128)S(1)} %get-tuple-element.181) | copy-start | bytes 3076
  26.9 4.6 %copy-start.37 = (f32[1,256]{1,0:T(1,128)}, f32[1,256]{1,0:T(1,128)S(1)}, u32[]{:S(2)}) copy-start(f32[1,256]{1,0:T(1,128)S(1)} %get-tuple-element.182) | copy-start | bytes 3076
  26.9 4.6 %copy-start.38 = (f32[1,256]{1,0:T(1,128)}, f32[1,256]{1,0:T(1,128)S(1)}, u32[]{:S(2)}) copy-start(f32[1,256]{1,0:T(1,128)S(1)} %get-tuple-element.183) | copy-start | bytes 3076
  46.4 53.5 %collective-permute-start.6 = (f32[18,3,256]{2,1,0:T(4,128)}, f32[18,3,256]{2,1,0:T(4,128)S(1)}, u32[]{:S(2)}, u32[]{:S(2)}) collective-permute-start(f32[18,3,256]{2,1,0:T(4,128)} %get-tuple-element.126), channel_id=1, source_target_pairs={{0,1},{1,2},{2,3},{3,0},{4,5},{5,6},{6,7},{7,4},{8,9},{9,10},{10,1... | collective-permute-start | bytes 165896 | tf_op jit(solution)/shard_map/ppermute | solution.py:17
  50.5 45.2 %copy-start.4 = (bf16[1024,256]{1,0:T(8,128)(2,1)S(1)}, bf16[1024,256]{1,0:T(8,128)(2,1)}, u32[]{:S(2)}) copy-start(bf16[1024,256]{1,0:T(8,128)(2,1)} %param.19) | copy-start | bytes 1572868
  97.4 5.1 %collective-permute-start.7 = (f32[18,3,256]{2,1,0:T(4,128)S(1)}, f32[18,3,256]{2,1,0:T(4,128)S(1)}, u32[]{:S(2)}, u32[]{:S(2)}) collective-permute-start(f32[18,3,256]{2,1,0:T(4,128)S(1)} %copy-done.5), channel_id=1, source_target_pairs={{1,0},{2,1},{3,2},{0,3},{5,4},{6,5},{7,6},{4,7},{9,8},{10,9},{11,1... | collective-permute-start | bytes 165896 | tf_op jit(solution)/shard_map/ppermute | solution.py:19
  102.8 8.1 %collective-permute-start.8 = (f32[3,24,256]{2,1,0:T(8,128)S(1)}, f32[3,24,256]{2,1,0:T(8,128)S(1)}, u32[]{:S(2)}, u32[]{:S(2)}) collective-permute-start(f32[3,24,256]{2,1,0:T(8,128)S(1)} %rev.15), channel_id=1, source_target_pairs={{0,2},{1,3},{2,0},{3,1},{4,6},{5,7},{6,4},{7,5},{8,10},{9,11},{10,... | collective-permute-start | bytes 221192 | tf_op jit(solution)/shard_map/ppermute | solution.py:28
  104.4 6.5 %collective-permute-start.9 = (f32[3,24,256]{2,1,0:T(8,128)S(1)}, f32[3,24,256]{2,1,0:T(8,128)S(1)}, u32[]{:S(2)}, u32[]{:S(2)}) collective-permute-start(f32[3,24,256]{2,1,0:T(8,128)S(1)} %get-tuple-element.127), channel_id=1, source_target_pairs={{0,4},{4,8},{8,12},{12,16},{16,20},{20,24},{24,28},{1,5},{5,9},{9,... | collective-permute-start | bytes 221192 | tf_op jit(solution)/shard_map/ppermute | solution.py:17
  106.3 6.7 %collective-permute-start.11 = (f32[3,24,256]{2,1,0:T(8,128)S(1)}, f32[3,24,256]{2,1,0:T(8,128)S(1)}, u32[]{:S(2)}, u32[]{:S(2)}) collective-permute-start(f32[3,24,256]{2,1,0:T(8,128)S(1)} %get-tuple-element.128), channel_id=1, source_target_pairs={{4,0},{8,4},{12,8},{16,12},{20,16},{24,20},{28,24},{5,1},{9,5},{13... | collective-permute-start | bytes 221192 | tf_op jit(solution)/shard_map/ppermute | solution.py:19
  107.6 5.4 %collective-permute-start.10 = (f32[3,24,256]{2,1,0:T(8,128)S(1)}, f32[3,24,256]{2,1,0:T(8,128)S(1)}, u32[]{:S(2)}, u32[]{:S(2)}) collective-permute-start(f32[3,24,256]{2,1,0:T(8,128)S(1)} %rev.16), channel_id=1, source_target_pairs={{0,2},{1,3},{2,0},{3,1},{4,6},{5,7},{6,4},{7,5},{8,10},{9,11},{10,... | collective-permute-start | bytes 221192 | tf_op jit(solution)/shard_map/ppermute | solution.py:28
  (12 other events, 16.2 us)
Sparse Core Ops, SparseCore 0:
  40.6 141.9 reduce-scatter.3
where the time goes:
time: 190 us; the launch traced here: 189 us
  waiting for transfers between devices  79.9 us (42%)
  blocking collectives  41.8 us (22%)
  starting transfers between devices  22.4 us (12%)
  between operations  15 us (8%)
  other arithmetic  14.8 us (8%)
  local copies, waits for them, and re-layouts  11.5 us (6%)
  matrix products  4.02 us (2%)
    unnamed x2, waiting for transfers between devices  68.9 us
    psum x1, blocking collectives, body(): tap_total, gain_total = lax.psum((tap_local, gain_local), ('lat', 'lon'))  41.8 us
    ppermute x4, starting transfers between devices, padded_2(): lax.ppermute(tail, axis, [(i, (i + 1) % count) for i in range(ends)])  7.88 us
    ppermute x4, starting transfers between devices, padded_2(): lax.ppermute(head, axis, [((i + 1) % count, i) for i in range(ends)])  7.87 us
    ppermute x4, starting transfers between devices, shifted(): lax.ppermute(value, axis, [(i, (i + by) % peers) for i in range(peers)])  6.65 us
    ppermute x4, waiting for transfers between devices, shifted(): lax.ppermute(value, axis, [(i, (i + by) % peers) for i in range(peers)])  6.36 us
    add x1, other arithmetic, adjoint_taps(): running + depthwise[7 * row_off + col_off] * padded[6 - row_off:12 - row_...  4.33 us
    unnamed x95, local copies, waits for them, and re-layouts  3.86 us
  transfers between devices with their start and end apart: 13, of which 7 were waited for; matrix products, arithmetic and copies ran while one was open for 9% of the time, Pallas kernels for 0%

commit v1 on v0

v1 whole, which is shorter than its diff:
```python
import functools
import math

import jax
import jax.numpy as jnp
from jax import lax
from jax.experimental import pallas as pl
from jax.experimental.pallas import tpu as pltpu
from jax.sharding import PartitionSpec as P

MESH = pl.DeviceIdType.MESH
F32 = jnp.float32
BF16 = jnp.bfloat16
SIDE = 8
CHUNK = 256
TAP_HALF = 32


def dot(left, right, dims):
    return lax.dot_general(left, right, (dims, ((), ())), preferred_element_type=F32)


def bits_of(size):
    return size.bit_length() - 1


def kernel(
    n_lat, n_lon,
    state, cot, taps, gain, w_in, w_out,
    out, gin, wgrad, gtaps, ggain,
    ext, rims, shifts, gext, grims, gshifts, conv, centred_s, istd_s, normed_s, cot_s,
    branch_s, gnorm_s, turned, local_w, core_w, tap_mine, tap_far, tap_sum, tap_done,
    r_own, r_got, l_own, l_got, t_got,
    halo_send, halo_recv, core_send, core_recv, ring_send, ring_recv, tap_send, tap_recv,
):
    height, width, channels = state.shape
    cells = height * width
    units = w_in.shape[1]
    rows = units // (n_lat * n_lon)
    block = n_lon * rows
    half_blocks = n_lat // 2
    lat, lon = lax.axis_index("lat"), lax.axis_index("lon")
    first, last = lat == 0, lat == n_lat - 1
    core = lax.rem(lat, 2)

    def wrap(value):
        return lax.rem(value + 2 * n_lon, n_lon)

    up_lat = jnp.where(first, 0, lat - 1)
    down_lat = jnp.where(last, n_lat - 1, lat + 1)
    up_off = jnp.where(first, n_lon // 2, 0)
    down_off = jnp.where(last, n_lon // 2, 0)
    up_side = jnp.where(first, 0, 1)
    down_side = jnp.where(last, 1, 0)

    def flip_bit(index, bit):
        size = 1 << bit
        mine = lax.rem(lax.div(index, size), 2)
        return index + size - 2 * size * mine, mine

    def lat_peer(bit):
        peer, mine = flip_bit(lat, bit)
        return (peer, lon), mine

    def lon_peer(bit):
        peer, mine = flip_bit(lon, bit)
        return (lat, peer), mine

    core_peer, _ = lat_peer(0)

    peers = []
    for side in (-1, 0, 1):
        peers.append((up_lat, wrap(lon + up_off + side)))
        peers.append((down_lat, wrap(lon + down_off + side)))
    peers.append((lat, wrap(lon - 1)))
    peers.append((lat, wrap(lon + 1)))
    for bit in range(bits_of(n_lat)):
        peers.append(lat_peer(bit)[0])
    for bit in range(bits_of(n_lon)):
        peers.append(lon_peer(bit)[0])
    barrier = pltpu.get_barrier_semaphore()
    for peer in peers:
        pl.semaphore_signal(barrier, inc=1, device_id=peer, device_id_type=MESH)
    pl.semaphore_wait(barrier, len(peers))

    def remote(source, target, send, recv, peer):
        return pltpu.make_async_remote_copy(
            src_ref=source, dst_ref=target, send_sem=send, recv_sem=recv,
            device_id=peer, device_id_type=MESH,
        )

    spans = ((-1, 0, SIDE), (0, 0, width), (1, width - SIDE, SIDE))
    places = ((-1, SIDE + width), (0, SIDE), (1, 0))

    def halo_copies(stage, source, whole, rim):
        copies = []
        for number, ((side, start, count), (_, place)) in enumerate(zip(spans, places)):
            for end, (peer_lat, off, slot) in enumerate(
                ((up_lat, up_off, up_side), (down_lat, down_off, down_side))
            ):
                begin = 0 if end == 0 else height - 3
                copies.append(
                    remote(
                        source.at[pl.ds(begin, 3), pl.ds(start, count)],
                        rim.at[slot, :, pl.ds(place, count)],
                        halo_send.at[stage, 2 * number + end],
                        halo_recv.at[stage, 2 * number + slot],
                        (peer_lat, wrap(lon + off + side)),
                    )
                )
        copies.append(
            remote(
                source.at[:, pl.ds(0, SIDE)], whole.at[pl.ds(3, height), pl.ds(SIDE + width, SIDE)],
                halo_send.at[stage, 6], halo_recv.at[stage, 6], (lat, wrap(lon - 1)),
            )
        )
        copies.append(
            remote(
                source.at[:, pl.ds(width - SIDE, SIDE)], whole.at[pl.ds(3, height), pl.ds(0, SIDE)],
                halo_send.at[stage, 7], halo_recv.at[stage, 7], (lat, wrap(lon + 1)),
            )
        )
        return copies

    def finish_halo(stage, source, whole, rim, shifted):
        copies = halo_copies(stage, source, whole, rim)
        for copy in copies:
            copy.wait_send()
        for copy in copies[6:]:
            copy.wait_recv()
        for number, ((_, start, count), (_, place)) in enumerate(zip(spans, places)):
            for slot in range(2):
                remote(
                    source.at[pl.ds(0, 3), pl.ds(start, count)],
                    rim.at[slot, :, pl.ds(place, count)],
                    halo_send.at[stage, 2 * number + slot],
                    halo_recv.at[stage, 2 * number + slot],
                    (lat, wrap(lon + 1)),
                ).wait_recv()
        for row in range(3):
            whole[row] = jnp.where(first, rim[0, 2 - row], rim[0, row])
            whole[height + 3 + row] = jnp.where(last, rim[1, 2 - row], rim[1, row])

        def shift_row(row, carry):
            for col in range(7):
                shifted[col, row] = whole[row, pl.ds(SIDE - 3 + col, width), :]
            return carry

        lax.fori_loop(0, height + 6, shift_row, 0)

    for copy in halo_copies(0, state, ext, rims):
        copy.start()

    ext[pl.ds(3, height), pl.ds(SIDE, width), :] = state[...]
    cot_s[...] = cot[...].astype(F32).reshape(cells, channels).astype(BF16)
    branch_s[...] = jnp.zeros_like(branch_s)
    gnorm_s[...] = jnp.zeros_like(gnorm_s)
    for row in range(7):
        for col in range(7):
            plain = taps[pl.ds(48 - 7 * row - col, 1), :]
            mirrored = taps[pl.ds(7 * row + 6 - col, 1), :]
            spot = pl.ds(7 * row + col, 1)
            turned[0, spot, :] = jnp.where(first, mirrored, plain)
            turned[1, spot, :] = plain
            turned[2, spot, :] = jnp.where(last, mirrored, plain)

    finish_halo(0, state, ext, rims, shifts)

    def conv_row(index, carry):
        total = jnp.zeros((width, channels), F32)
        for row in range(7):
            for col in range(7):
                total = total + shifts[col, index + row] * taps[pl.ds(7 * row + col, 1), :]
        conv[index] = total
        return carry

    lax.fori_loop(0, height, conv_row, 0)

    flat = conv[...].reshape(cells, channels)
    raw = flat - jnp.mean(flat, axis=-1, keepdims=True)
    inv_std = 1.0 / jnp.sqrt(jnp.mean(raw * raw, axis=-1, keepdims=True) + 1e-06)
    centred = raw * inv_std
    istd_s[...] = inv_std
    centred_s[...] = centred
    normed_s[...] = (centred * gain[...]).astype(BF16)

    per_chunk = CHUNK // (2 * block)

    def core_copy(chunk):
        span = pl.ds(chunk * per_chunk, per_chunk)
        return remote(
            local_w.at[span, 1 - core], core_w.at[span],
            core_send.at[chunk], core_recv.at[chunk], core_peer,
        )

    def unit_chunk(chunk, carry):
        span = pl.ds(pl.multiple_of(chunk * CHUNK, CHUNK), CHUNK)
        into = w_in[:, span]
        outof = w_out[span, :]
        pre = dot(normed_s[...], into, ((1,), (0,)))
        share = 0.5 * (1.0 + lax.erf(pre * 0.7071067811865476))
        hidden = (pre * share).astype(BF16)
        slope = share + pre * jnp.exp(-0.5 * pre * pre) * 0.3989422804014327
        grad_pre = (dot(cot_s[...], outof, ((1,), (1,))) * slope).astype(BF16)
        left = dot(grad_pre, normed_s[...], ((0,), (0,)))
        right = dot(hidden, cot_s[...], ((0,), (0,)))
        blocks = pl.ds(chunk * per_chunk, per_chunk)
        local_w[blocks, :, :, pl.ds(0, channels)] = left.reshape(per_chunk, 2, block, channels)
        local_w[blocks, :, :, pl.ds(channels, channels)] = right.reshape(
            per_chunk, 2, block, channels
        )
        core_copy(chunk).start()
        branch_s[...] += dot(hidden, outof, ((1,), (0,)))
        gnorm_s[...] += dot(grad_pre, into, ((1,), (1,)))
        return carry

    lax.fori_loop(0, units // CHUNK, unit_chunk, 0)

    gnorm = gnorm_s[...]
    centred = centred_s[...]
    scaled = gnorm * gain[...]
    grad_conv = istd_s[...] * (
        scaled
        - jnp.mean(scaled, axis=-1, keepdims=True)
        - centred * jnp.mean(scaled * centred, axis=-1, keepdims=True)
    )
    conv[...] = grad_conv.reshape(height, width, channels)
    for copy in halo_copies(1, conv, gext, grims):
        copy.start()
    gext[pl.ds(3, height), pl.ds(SIDE, width), :] = conv[...]
    tap_mine[1, pl.ds(TAP_HALF // 2, TAP_HALF // 2), :] = jnp.zeros((TAP_HALF // 2, channels), F32)
    tap_mine[1, pl.ds(49 - TAP_HALF, 1), :] = jnp.sum(gnorm * centred, axis=0, keepdims=True)

    lat_bits = list(range(1, bits_of(n_lat)))
    lon_bits = list(range(bits_of(n_lon)))
    r_steps = [("lat", bit) for bit in lat_bits] + [("lon", bit) for bit in lon_bits]
    l_steps = [("lat", bit) for bit in lat_bits[::-1]] + [("lon", bit) for bit in lon_bits]

    def peer_of(step):
        return lat_peer(step[1]) if step[0] == "lat" else lon_peer(step[1])

    def ring_copy(stream, own, got, steps, number):
        peer, mine = peer_of(steps[number])
        low = stream == 0 or steps[number][0] == "lon"
        source = own[number].at[:, 1 - mine] if low else own[number].at[1 - mine]
        return remote(
            source, got[number], ring_send.at[stream, number], ring_recv.at[stream, number], peer
        )

    def store_own(own, number, index, value, steps, stream):
        step = steps[number]
        low = stream == 0 or step[0] == "lon"
        if low:
            own[number][index // 2, index % 2] = value
        else:
            count = own[number].shape[1]
            own[number][index // count, index % count] = value

    def place(own, number, steps, stream, pieces):
        if steps[number][0] == "lon" and (number == 0 or steps[number - 1][0] == "lat"):
            (piece,) = pieces
            pieces = [piece[rows * part : rows * (part + 1)] for part in range(n_lon)]
        for index, value in enumerate(pieces):
            store_own(own, number, index, value, steps, stream)

    def ring_sum(stream, own, got, steps, number):
        _, mine = peer_of(steps[number])
        low = stream == 0 or steps[number][0] == "lon"
        pieces = []
        for index in range(got[number].shape[0]):
            kept = own[number][index, mine] if low else own[number][mine, index]
            pieces.append(kept + got[number][index])
        return pieces

    for chunk in range(units // CHUNK):
        core_copy(chunk).wait()
    for stream, own, got, steps, begin in (
        (0, r_own, r_got, r_steps, channels), (1, l_own, l_got, l_steps, 0)
    ):
        pieces = [
            local_w[index, core, :, pl.ds(begin, channels)]
            + core_w[index, :, pl.ds(begin, channels)]
            for index in range(half_blocks)
        ]
        place(own, 0, steps, stream, pieces)
        ring_copy(stream, own, got, steps, 0).start()

    out[...] = (
        state[...] + branch_s[...].reshape(height, width, channels)
    ).astype(BF16)

    def tap_row(index, carry):
        row, col = lax.div(index, 7), lax.rem(index, 7)
        total = jnp.zeros((width, channels), F32)
        for line in range(height):
            total = total + shifts[col, row + line] * conv[line]
        tap_mine[lax.div(index, TAP_HALF), pl.ds(lax.rem(index, TAP_HALF), 1), :] = jnp.sum(
            total, axis=0, keepdims=True
        )
        return carry

    lax.fori_loop(0, 49, tap_row, 0)
    tap_first = remote(
        tap_mine.at[1 - core], tap_far, tap_send.at[0], tap_recv.at[0], core_peer
    )
    tap_first.start()

    finish_halo(1, conv, gext, grims, gshifts)

    def adjoint_row(index, carry):
        total = jnp.zeros((width, channels), F32)
        for row in range(7):
            line = index + row
            kind = jnp.where(line < 3, 0, jnp.where(line >= height + 3, 2, 1))
            for col in range(7):
                total = total + gshifts[col, line] * turned[kind, pl.ds(7 * row + col, 1), :]
        ext[index, pl.ds(0, width), :] = total
        return carry

    lax.fori_loop(0, height, adjoint_row, 0)
    gin[...] = (cot[...].astype(F32) + ext[pl.ds(0, height), pl.ds(0, width), :]).astype(BF16)

    tap_first.wait()
    tap_sum[0] = tap_mine[core] + tap_far[...]

    def tap_copy(number):
        peer, _ = peer_of(r_steps[number])
        return remote(
            tap_sum.at[number], t_got.at[number],
            tap_send.at[1 + number], tap_recv.at[1 + number], peer,
        )

    scale = 1.0 / math.sqrt(cells * n_lat * n_lon)
    tap_copy(0).start()
    count = len(r_steps)
    for number in range(count):
        for stream, own, got, steps, begin in (
            (0, r_own, r_got, r_steps, channels), (1, l_own, l_got, l_steps, 0)
        ):
            ring_copy(stream, own, got, steps, number).wait()
            pieces = ring_sum(stream, own, got, steps, number)
            if number < count - 1:
                place(own, number + 1, steps, stream, pieces)
                ring_copy(stream, own, got, steps, number + 1).start()
            else:
                wgrad[:, pl.ds(begin, channels)] = pieces[0] * scale
        tap_copy(number).wait()
        total = tap_sum[number] + t_got[number]
        if number < count - 1:
            tap_sum[number + 1] = total
            tap_copy(number + 1).start()
        else:
            tap_done[core] = total * scale
    tap_last = remote(
        tap_done.at[core], tap_done.at[core],
        tap_send.at[1 + count], tap_recv.at[1 + count], core_peer,
    )
    tap_last.start()
    tap_last.wait()
    gtaps[pl.ds(0, TAP_HALF), :] = tap_done[0]
    gtaps[pl.ds(TAP_HALF, 49 - TAP_HALF), :] = tap_done[1, pl.ds(0, 49 - TAP_HALF), :]
    ggain[...] = tap_done[1, pl.ds(49 - TAP_HALF, 1), :]


def ring_shapes(n_lat, n_lon, rows, channels, low_first):
    own, got = [], []
    left = n_lat // 2
    while left > 1:
        pair = (left // 2, 2) if low_first else (2, left // 2)
        own.append(pltpu.VMEM(pair + (n_lon * rows, channels), F32))
        got.append(pltpu.VMEM((left // 2, n_lon * rows, channels), F32))
        left //= 2
    left = n_lon
    while left > 1:
        own.append(pltpu.VMEM((left // 2, 2, rows, channels), F32))
        got.append(pltpu.VMEM((left // 2, rows, channels), F32))
        left //= 2
    return own, got


def solution(mesh):
    n_lat, n_lon = mesh.shape["lat"], mesh.shape["lon"]

    def body(state, cot, taps, gain, w_in, w_out):
        height, width, channels = state.shape
        units = w_in.shape[1]
        cells = height * width
        rows = units // (n_lat * n_lon)
        block = n_lon * rows
        r_own, r_got = ring_shapes(n_lat, n_lon, rows, channels, True)
        l_own, l_got = ring_shapes(n_lat, n_lon, rows, channels, False)
        steps = len(r_own)
        wide = width + 2 * SIDE
        vmem = pl.BlockSpec(memory_space=pltpu.VMEM)
        dma = pltpu.SemaphoreType.DMA
        results = pl.pallas_call(
            functools.partial(kernel, n_lat, n_lon),
            out_shape=(
                jax.ShapeDtypeStruct((height, width, channels), BF16),
                jax.ShapeDtypeStruct((height, width, channels), BF16),
                jax.ShapeDtypeStruct((rows, 2 * channels), F32),
                jax.ShapeDtypeStruct((49, channels), F32),
                jax.ShapeDtypeStruct((1, channels), F32),
            ),
            in_specs=[vmem] * 6,
            out_specs=[vmem] * 5,
            scratch_shapes=[
                pltpu.VMEM((height + 6, wide, channels), F32),
                pltpu.VMEM((2, 3, wide, channels), F32),
                pltpu.VMEM((7, height + 6, width, channels), F32),
                pltpu.VMEM((height + 6, wide, channels), F32),
                pltpu.VMEM((2, 3, wide, channels), F32),
                pltpu.VMEM((7, height + 6, width, channels), F32),
                pltpu.VMEM((height, width, channels), F32),
                pltpu.VMEM((cells, channels), F32),
                pltpu.VMEM((cells, 1), F32),
                pltpu.VMEM((cells, channels), BF16),
                pltpu.VMEM((cells, channels), BF16),
                pltpu.VMEM((cells, channels), F32),
                pltpu.VMEM((cells, channels), F32),
                pltpu.VMEM((3, 49, channels), F32),
                pltpu.VMEM((n_lat // 2, 2, block, 2 * channels), F32),
                pltpu.VMEM((n_lat // 2, block, 2 * channels), F32),
                pltpu.VMEM((2, TAP_HALF, channels), F32),
                pltpu.VMEM((TAP_HALF, channels), F32),
                pltpu.VMEM((steps, TAP_HALF, channels), F32),
                pltpu.VMEM((2, TAP_HALF, channels), F32),
                r_own, r_got, l_own, l_got,
                pltpu.VMEM((steps, TAP_HALF, channels), F32),
                dma((2, 8)), dma((2, 8)), dma((units // CHUNK,)), dma((units // CHUNK,)),
                dma((2, steps)), dma((2, steps)), dma((steps + 2,)), dma((steps + 2,)),
            ],
            compiler_params=pltpu.CompilerParams(
                collective_id=0, has_side_effects=True, vmem_limit_bytes=48 * 1024 * 1024
            ),
            name="block",
        )(state, cot, taps, gain.reshape(1, channels), w_in, w_out)
        out, gin, wgrad, gtaps, ggain = results
        return out, gin, wgrad, gtaps, ggain.reshape(channels)

    placed = (P("lat", "lon", None), P("lat", "lon", None), P(), P(), P(), P())
    return jax.shard_map(
        body,
        mesh=mesh,
        in_specs=placed,
        out_specs=(P("lat", "lon", None), P("lat", "lon", None), P(("lat", "lon"), None), P(), P()),
        check_vma=False,
    )
```

time: 190 us -> 55.7 us (0.29)
  the two profiles are of different devices: /device:TPU:0 before, /device:TPU:19 now
where the time goes in v1:
time: 55.7 us; the launch traced here: 55.4 us
  Pallas kernels  46.1 us (83%)
  local copies, waits for them, and re-layouts  8.58 us (15%)
  between operations  0.66 us (1%)
    pallas_call x1, Pallas kernels, body(): pl.pallas_call(functools.partial(kernel, n_lat, n_lon), out_shape=(jax.Sh...  46.1 us
    unnamed x17, local copies, waits for them, and re-layouts  8.58 us

profile of v1, /device:TPU:19, one launch (start us, length us, event | category | flops | bytes accessed | tf_op | source)
XLA Modules:
  0.0 55.4 jit_solution(2712482646343261993)
XLA Ops:
  0.6 0.0 copy-start.5
  0.6 0.7 %copy-done.5 = f32[256]{0:T(256)S(1)} copy-done((f32[256]{0:T(256)S(1)}, f32[256]{0:T(256)}, u32[]{:S(2)}) %copy-start.5) | copy-done | bytes 1048
  1.3 0.0 copy-start
  1.3 1.0 %copy-done = bf16[256,1024]{1,0:T(8,128)(2,1)S(1)} copy-done((bf16[256,1024]{1,0:T(8,128)(2,1)S(1)}, bf16[256,1024]{1,0:T(8,128)(2,1)}, u32[]{:S(2)}) %copy-start) | copy-done | bytes 524312
  2.4 0.0 copy-start.1
  2.4 1.0 %copy-done.1 = bf16[1024,256]{1,0:T(8,128)(2,1)S(1)} copy-done((bf16[1024,256]{1,0:T(8,128)(2,1)S(1)}, bf16[1024,256]{1,0:T(8,128)(2,1)}, u32[]{:S(2)}) %copy-start.1) | copy-done | bytes 524312
  3.4 0.0 copy-start.2
  3.4 1.0 %copy-done.2 = f32[12,24,256]{2,1,0:T(8,128)S(1)} copy-done((f32[12,24,256]{2,1,0:T(8,128)S(1)}, f32[12,24,256]{2,1,0:T(8,128)}, u32[]{:S(2)}) %copy-start.2) | copy-done | bytes 294936
  4.4 0.0 copy-start.3
  4.4 0.9 %copy-done.3 = bf16[12,24,256]{2,1,0:T(8,128)(2,1)S(1)} copy-done((bf16[12,24,256]{2,1,0:T(8,128)(2,1)S(1)}, bf16[12,24,256]{2,1,0:T(8,128)(2,1)}, u32[]{:S(2)}) %copy-start.3) | copy-done | bytes 147480
  5.3 0.0 copy-start.4
  5.3 0.8 %copy-done.4 = f32[49,256]{1,0:T(8,128)S(1)} copy-done((f32[49,256]{1,0:T(8,128)S(1)}, f32[49,256]{1,0:T(8,128)}, u32[]{:S(2)}) %copy-start.4) | copy-done | bytes 50200
  6.1 46.1 %block.1 = (bf16[12,24,256]{2,1,0:T(8,128)(2,1)S(1)}, bf16[12,24,256]{2,1,0:T(8,128)(2,1)S(1)}, f32[32,512]{1,0:T(8,128)S(1)}, f32[49,256]{1,0:T(8,128)S(1)}, f32[1,256]{1,0:T(1,128)S(1)}) custom-call(f32[12,24,256]{2,1,0:T(8,128)S(1)} %copy-done.2, bf16[12,24,256]{2,1,0:T(8,128)(2,1)S(1)} %copy-done.3, f32[49,256]{1,0:T(8,128)S(1)} %copy-done.4, ...), custom_call_target="tpu_custom_call" | custom-call | tf_op jit(solution)/shard_map/block/pallas_call | solution.py:396
  52.2 0.7 %copy.16 = bf16[12,24,256]{2,1,0:T(8,128)(2,1)} copy(bf16[12,24,256]{2,1,0:T(8,128)(2,1)S(1)} %get-tuple-element.20) | data formatting | bytes 294912
  52.9 0.7 %copy.17 = bf16[12,24,256]{2,1,0:T(8,128)(2,1)} copy(bf16[12,24,256]{2,1,0:T(8,128)(2,1)S(1)} %get-tuple-element.21) | data formatting | bytes 294912
  53.5 0.6 %copy.18 = f32[32,512]{1,0:T(8,128)} copy(f32[32,512]{1,0:T(8,128)S(1)} %get-tuple-element.22) | data formatting | bytes 131072
  54.2 0.6 %copy.19 = f32[49,256]{1,0:T(8,128)} copy(f32[49,256]{1,0:T(8,128)S(1)} %get-tuple-element.23) | data formatting | bytes 100352
  54.8 0.6 %copy.20 = f32[256]{0:T(256)} copy(f32[256]{0:T(256)S(1)} %bitcast.2) | data formatting | bytes 2048
Async XLA Ops:
  0.6 0.7 %copy-start.5 = (f32[256]{0:T(256)S(1)}, f32[256]{0:T(256)}, u32[]{:S(2)}) copy-start(f32[256]{0:T(256)} %param.9) | copy-start | bytes 3076
  1.3 1.0 %copy-start = (bf16[256,1024]{1,0:T(8,128)(2,1)S(1)}, bf16[256,1024]{1,0:T(8,128)(2,1)}, u32[]{:S(2)}) copy-start(bf16[256,1024]{1,0:T(8,128)(2,1)} %w_in.1) | copy-start | bytes 1572868
  2.4 1.0 %copy-start.1 = (bf16[1024,256]{1,0:T(8,128)(2,1)S(1)}, bf16[1024,256]{1,0:T(8,128)(2,1)}, u32[]{:S(2)}) copy-start(bf16[1024,256]{1,0:T(8,128)(2,1)} %w_out.1) | copy-start | bytes 1572868
  3.4 1.0 %copy-start.2 = (f32[12,24,256]{2,1,0:T(8,128)S(1)}, f32[12,24,256]{2,1,0:T(8,128)}, u32[]{:S(2)}) copy-start(f32[12,24,256]{2,1,0:T(8,128)} %state.1) | copy-start | bytes 884740
  4.4 0.9 %copy-start.3 = (bf16[12,24,256]{2,1,0:T(8,128)(2,1)S(1)}, bf16[12,24,256]{2,1,0:T(8,128)(2,1)}, u32[]{:S(2)}) copy-start(bf16[12,24,256]{2,1,0:T(8,128)(2,1)} %cot.1) | copy-start | bytes 442372
  5.3 0.8 %copy-start.4 = (f32[49,256]{1,0:T(8,128)S(1)}, f32[49,256]{1,0:T(8,128)}, u32[]{:S(2)}) copy-start(f32[49,256]{1,0:T(8,128)} %taps.1) | copy-start | bytes 150532

commit v2 on v1

v2 whole, which is shorter than its diff:
```python
import functools
import math

import jax
import jax.numpy as jnp
from jax import lax
from jax.experimental import pallas as pl
from jax.experimental.pallas import tpu as pltpu
from jax.sharding import PartitionSpec as P

MESH = pl.DeviceIdType.MESH
F32 = jnp.float32
BF16 = jnp.bfloat16
SIDE = 8
TAP_HALF = 32


def dot(left, right, dims):
    return lax.dot_general(left, right, (dims, ((), ())), preferred_element_type=F32)


def kernel(
    n_lat, n_lon,
    state_h, cot_h, taps_h, gain_h, w_in_h, w_out_h,
    out, gin, wgrad, gtaps, ggain,
    state, cot, taps, gain, w_in, w_out,
    ext, rims, shifts, gext, grims, gshifts, conv, centred_s, istd_s, normed_s, cot_s,
    branch_s, gnorm_s, ghid_s, turned, local_w, core_w, pair_own, pair_got, group_own, group_got,
    tap_mine, tap_far, tap_chip, tap_group, tap_done,
    load_sem, halo_send, halo_recv, core_send, core_recv, pair_send, pair_recv,
    group_send, group_recv, tap_send, tap_recv, spread_send, spread_recv,
):
    loads = [
        pltpu.make_async_copy(source, target, load_sem.at[number])
        for number, (source, target) in enumerate(
            (
                (state_h, state), (cot_h, cot), (taps_h, taps),
                (gain_h, gain), (w_in_h, w_in), (w_out_h, w_out),
            )
        )
    ]
    for load in loads:
        load.start()
    height, width, channels = state.shape
    cells = height * width
    units = w_in.shape[1]
    rows = units // (n_lat * n_lon)
    block = n_lon * rows
    subs = n_lat // 8
    members = subs * n_lon
    chunk_rows = units // 4
    lat, lon = lax.axis_index("lat"), lax.axis_index("lon")
    first, last = lat == 0, lat == n_lat - 1
    core = lax.rem(lat, 2)

    def wrap(value):
        return lax.rem(value + 2 * n_lon, n_lon)

    up_lat = jnp.where(first, 0, lat - 1)
    down_lat = jnp.where(last, n_lat - 1, lat + 1)
    up_off = jnp.where(first, n_lon // 2, 0)
    down_off = jnp.where(last, n_lon // 2, 0)
    up_side = jnp.where(first, 0, 1)
    down_side = jnp.where(last, 1, 0)

    high_y = lax.div(lat, n_lat // 2)
    high_x = lax.rem(lax.div(lat, n_lat // 4), 2)
    base = lat - lax.rem(lat, n_lat // 4) + core
    member = lax.rem(lax.div(lat, 2), subs) * n_lon + lon
    core_peer = (lat + 1 - 2 * core, lon)

    def chip_peer(code):
        there = lat
        if code & 1:
            there = there + (n_lat // 4) * (1 - 2 * high_x)
        if code & 2:
            there = there + (n_lat // 2) * (1 - 2 * high_y)
        return there, lon

    def group_peer(step):
        index = lax.rem(member + step, members)
        return index, (base + 2 * lax.div(index, n_lon), lax.rem(index, n_lon))

    peers = []
    for side in (-1, 0, 1):
        peers.append((up_lat, wrap(lon + up_off + side)))
        peers.append((down_lat, wrap(lon + down_off + side)))
    peers.append((lat, wrap(lon - 1)))
    peers.append((lat, wrap(lon + 1)))
    peers.append(core_peer)
    for code in range(1, 4):
        peers.append(chip_peer(code))
    for step in range(1, members):
        peers.append(group_peer(step)[1])
    barrier = pltpu.get_barrier_semaphore()
    for peer in peers:
        pl.semaphore_signal(barrier, inc=1, device_id=peer, device_id_type=MESH)
    pl.semaphore_wait(barrier, len(peers))

    def remote(source, target, send, recv, peer):
        return pltpu.make_async_remote_copy(
            src_ref=source, dst_ref=target, send_sem=send, recv_sem=recv,
            device_id=peer, device_id_type=MESH,
        )

    spans = ((-1, 0, SIDE), (0, 0, width), (1, width - SIDE, SIDE))
    places = ((-1, SIDE + width), (0, SIDE), (1, 0))

    def halo_copies(stage, source, whole, rim):
        copies = []
        for number, ((side, start, count), (_, place)) in enumerate(zip(spans, places)):
            for end, (peer_lat, off, slot) in enumerate(
                ((up_lat, up_off, up_side), (down_lat, down_off, down_side))
            ):
                begin = 0 if end == 0 else height - 3
                copies.append(
                    remote(
                        source.at[pl.ds(begin, 3), pl.ds(start, count)],
                        rim.at[slot, :, pl.ds(place, count)],
                        halo_send.at[stage, 2 * number + end],
                        halo_recv.at[stage, 2 * number + slot],
                        (peer_lat, wrap(lon + off + side)),
                    )
                )
        copies.append(
            remote(
                source.at[:, pl.ds(0, SIDE)], whole.at[pl.ds(3, height), pl.ds(SIDE + width, SIDE)],
                halo_send.at[stage, 6], halo_recv.at[stage, 6], (lat, wrap(lon - 1)),
            )
        )
        copies.append(
            remote(
                source.at[:, pl.ds(width - SIDE, SIDE)], whole.at[pl.ds(3, height), pl.ds(0, SIDE)],
                halo_send.at[stage, 7], halo_recv.at[stage, 7], (lat, wrap(lon + 1)),
            )
        )
        return copies

    def finish_halo(stage, source, whole, rim, shifted):
        copies = halo_copies(stage, source, whole, rim)
        for copy in copies:
            copy.wait_send()
        for copy in copies[6:]:
            copy.wait_recv()
        for number, ((_, start, count), (_, place)) in enumerate(zip(spans, places)):
            for slot in range(2):
                remote(
                    source.at[pl.ds(0, 3), pl.ds(start, count)],
                    rim.at[slot, :, pl.ds(place, count)],
                    halo_send.at[stage, 2 * number + slot],
                    halo_recv.at[stage, 2 * number + slot],
                    (lat, wrap(lon + 1)),
                ).wait_recv()
        for row in range(3):
            whole[row] = jnp.where(first, rim[0, 2 - row], rim[0, row])
            whole[height + 3 + row] = jnp.where(last, rim[1, 2 - row], rim[1, row])

        def shift_row(row, carry):
            for col in range(7):
                shifted[col, row] = whole[row, pl.ds(SIDE - 3 + col, width), :]
            return carry

        lax.fori_loop(0, height + 6, shift_row, 0)

    for copy in halo_copies(0, state_h, ext, rims):
        copy.start()

    for load in loads:
        load.wait()
    ext[pl.ds(3, height), pl.ds(SIDE, width), :] = state[...]
    cot_s[...] = cot[...].astype(F32).reshape(cells, channels).astype(BF16)
    for chunk in range(4):
        ghid_s[chunk] = dot(
            cot_s[...], w_out[pl.ds(chunk * chunk_rows, chunk_rows), :], ((1,), (1,))
        )
    for row in range(7):
        for col in range(7):
            plain = taps[pl.ds(48 - 7 * row - col, 1), :]
            mirrored = taps[pl.ds(7 * row + 6 - col, 1), :]
            spot = pl.ds(7 * row + col, 1)
            turned[0, spot, :] = jnp.where(first, mirrored, plain)
            turned[1, spot, :] = plain
            turned[2, spot, :] = jnp.where(last, mirrored, plain)

    finish_halo(0, state_h, ext, rims, shifts)

    def conv_row(index, carry):
        total = jnp.zeros((width, channels), F32)
        for row in range(7):
            for col in range(7):
                total = total + shifts[col, index + row] * taps[pl.ds(7 * row + col, 1), :]
        conv[index] = total
        return carry

    lax.fori_loop(0, height, conv_row, 0)

    flat = conv[...].reshape(cells, channels)
    raw = flat - jnp.mean(flat, axis=-1, keepdims=True)
    inv_std = 1.0 / jnp.sqrt(jnp.mean(raw * raw, axis=-1, keepdims=True) + 1e-06)
    centred = raw * inv_std
    istd_s[...] = inv_std
    centred_s[...] = centred
    normed_s[...] = (centred * gain[...]).astype(BF16)

    def core_copy(turn):
        return remote(
            local_w.at[turn, :, 1 - core], core_w.at[turn],
            core_send.at[turn], core_recv.at[turn], core_peer,
        )

    def pair_copy(stream, slot):
        along_x = (stream == 0) == (slot < 2)
        return remote(
            pair_own.at[stream, slot], pair_got.at[stream, slot],
            pair_send.at[stream, slot], pair_recv.at[stream, slot],
            chip_peer(1) if along_x else chip_peer(2),
        )

    def core_sum(turn, stream):
        span = pl.ds(channels * (1 - stream), channels)
        return local_w[turn, :, core, :, span] + core_w[turn, :, :, span]

    def send_pair(stream, slot, value):
        pair_own[stream, slot] = value
        pair_copy(stream, slot).start()

    orders = ((1 - high_y, 1 - high_x), (high_y, 1 - high_x), (1 - high_y, high_x), (high_y, high_x))

    for turn, (part_y, part_x) in enumerate(orders):
        chunk = 2 * part_y + part_x
        span = pl.ds(pl.multiple_of(chunk * chunk_rows, chunk_rows), chunk_rows)
        into = w_in[:, span]
        outof = w_out[span, :]
        pre = dot(normed_s[...], into, ((1,), (0,)))
        share = 0.5 * (1.0 + lax.erf(pre * 0.7071067811865476))
        hidden = (pre * share).astype(BF16)
        slope = share + pre * jnp.exp(-0.5 * pre * pre) * 0.3989422804014327
        grad_pre = (ghid_s[chunk] * slope).astype(BF16)
        right = dot(hidden, cot_s[...], ((0,), (0,)))
        local_w[turn, :, :, :, pl.ds(channels, channels)] = right.reshape(subs, 2, block, channels)
        left = dot(grad_pre, normed_s[...], ((0,), (0,)))
        local_w[turn, :, :, :, pl.ds(0, channels)] = left.reshape(subs, 2, block, channels)
        core_copy(turn).start()
        branch = dot(hidden, outof, ((1,), (0,)))
        gnorm = dot(grad_pre, into, ((1,), (1,)))
        if turn == 0:
            branch_s[...] = branch
            gnorm_s[...] = gnorm
        else:
            branch_s[...] += branch
            gnorm_s[...] += gnorm
            core_copy(turn - 1).wait()
        if turn == 1:
            send_pair(0, 0, core_sum(0, 0))
            send_pair(1, 0, core_sum(0, 1))
        if turn == 2:
            send_pair(0, 1, core_sum(1, 0))
            pair_copy(1, 0).wait()
            send_pair(1, 2, core_sum(1, 1) + pair_got[1, 0])
        if turn == 3:
            send_pair(1, 1, core_sum(2, 1))
            pair_copy(0, 0).wait()
            send_pair(0, 2, core_sum(2, 0) + pair_got[0, 0])

    gnorm = gnorm_s[...]
    centred = centred_s[...]
    scaled = gnorm * gain[...]
    grad_conv = istd_s[...] * (
        scaled
        - jnp.mean(scaled, axis=-1, keepdims=True)
        - centred * jnp.mean(scaled * centred, axis=-1, keepdims=True)
    )
    conv[...] = grad_conv.reshape(height, width, channels)
    for copy in halo_copies(1, conv, gext, grims):
        copy.start()
    gext[pl.ds(3, height), pl.ds(SIDE, width), :] = conv[...]
    tap_mine[1, pl.ds(TAP_HALF // 2, TAP_HALF // 2), :] = jnp.zeros((TAP_HALF // 2, channels), F32)
    tap_mine[1, pl.ds(49 - TAP_HALF, 1), :] = jnp.sum(gnorm * centred, axis=0, keepdims=True)

    core_copy(3).wait()
    for stream in range(2):
        pair_copy(stream, 1).wait()
        pair_copy(stream, 2).wait()
        whole = core_sum(3, stream) + pair_got[stream, 1] + pair_got[stream, 2]
        for sub in range(subs):
            for part in range(n_lon):
                group_own[sub * n_lon + part, :, pl.ds(channels * (1 - stream), channels)] = whole[
                    sub, rows * part : rows * (part + 1)
                ]

    def group_copy(step):
        index, peer = group_peer(step)
        return remote(
            group_own.at[index], group_got.at[step - 1],
            group_send.at[step - 1], group_recv.at[step - 1], peer,
        )

    for step in range(1, members):
        group_copy(step).start()

    def tap_row(index, carry):
        row, col = lax.div(index, 7), lax.rem(index, 7)
        total = jnp.zeros((width, channels), F32)
        for line in range(height):
            total = total + shifts[col, row + line] * conv[line]
        tap_mine[lax.div(index, TAP_HALF), pl.ds(lax.rem(index, TAP_HALF), 1), :] = jnp.sum(
            total, axis=0, keepdims=True
        )
        return carry

    lax.fori_loop(0, 49, tap_row, 0)
    tap_first = remote(
        tap_mine.at[1 - core], tap_far, tap_send.at[0], tap_recv.at[0], core_peer
    )
    tap_first.start()

    out[...] = (
        state[...] + branch_s[...].reshape(height, width, channels)
    ).astype(BF16)
    finish_halo(1, conv, gext, grims, gshifts)

    tap_first.wait()
    quarter = 2 * high_y + high_x
    tap_chip[quarter] = tap_mine[core] + tap_far[...]

    def chip_copy(code):
        return remote(
            tap_chip.at[quarter], tap_chip.at[quarter],
            tap_send.at[1 + code], tap_recv.at[1 + code], chip_peer(code),
        )

    for code in range(1, 4):
        chip_copy(code).start()

    def adjoint_row(index, carry):
        total = jnp.zeros((width, channels), F32)
        for row in range(7):
            line = index + row
            kind = jnp.where(line < 3, 0, jnp.where(line >= height + 3, 2, 1))
            for col in range(7):
                total = total + gshifts[col, line] * turned[kind, pl.ds(7 * row + col, 1), :]
        ext[index, pl.ds(0, width), :] = total
        return carry

    lax.fori_loop(0, height // 2, adjoint_row, 0)

    for code in range(1, 4):
        chip_copy(code).wait()
    tap_group[member] = (tap_chip[0] + tap_chip[1]) + (tap_chip[2] + tap_chip[3])

    def spread_copy(step):
        _, peer = group_peer(step)
        return remote(
            tap_group.at[member], tap_group.at[member],
            spread_send.at[step - 1], spread_recv.at[step - 1], peer,
        )

    for step in range(1, members):
        spread_copy(step).start()

    lax.fori_loop(height // 2, height, adjoint_row, 0)

    scale = 1.0 / math.sqrt(cells * n_lat * n_lon)
    for step in range(1, members):
        group_copy(step).wait()
    total = group_own[member]
    for step in range(1, members):
        total = total + group_got[step - 1]
    wgrad[...] = total * scale

    for step in range(1, members):
        spread_copy(step).wait()
    total = tap_group[0]
    for step in range(1, members):
        total = total + tap_group[step]
    tap_done[core] = total * scale
    tap_last = remote(
        tap_done.at[core], tap_done.at[core], tap_send.at[1], tap_recv.at[1], core_peer
    )
    tap_last.start()
    gin[...] = (cot[...].astype(F32) + ext[pl.ds(0, height), pl.ds(0, width), :]).astype(BF16)
    tap_last.wait()
    gtaps[pl.ds(0, TAP_HALF), :] = tap_done[0]
    gtaps[pl.ds(TAP_HALF, 49 - TAP_HALF), :] = tap_done[1, pl.ds(0, 49 - TAP_HALF), :]
    ggain[...] = tap_done[1, pl.ds(49 - TAP_HALF, 1), :]


def solution(mesh):
    n_lat, n_lon = mesh.shape["lat"], mesh.shape["lon"]

    def body(state, cot, taps, gain, w_in, w_out):
        height, width, channels = state.shape
        units = w_in.shape[1]
        cells = height * width
        rows = units // (n_lat * n_lon)
        block = n_lon * rows
        subs = n_lat // 8
        members = subs * n_lon
        wide = width + 2 * SIDE
        vmem = pl.BlockSpec(memory_space=pltpu.VMEM)
        hbm = pl.BlockSpec(memory_space=pl.ANY)
        dma = pltpu.SemaphoreType.DMA
        args = (state, cot, taps, gain.reshape(1, channels), w_in, w_out)
        results = pl.pallas_call(
            functools.partial(kernel, n_lat, n_lon),
            out_shape=(
                jax.ShapeDtypeStruct((height, width, channels), BF16),
                jax.ShapeDtypeStruct((height, width, channels), BF16),
                jax.ShapeDtypeStruct((rows, 2 * channels), F32),
                jax.ShapeDtypeStruct((49, channels), F32),
                jax.ShapeDtypeStruct((1, channels), F32),
            ),
            in_specs=[hbm] * 6,
            out_specs=[vmem] * 5,
            scratch_shapes=[pltpu.VMEM(arg.shape, arg.dtype) for arg in args] + [
                pltpu.VMEM((height + 6, wide, channels), F32),
                pltpu.VMEM((2, 3, wide, channels), F32),
                pltpu.VMEM((7, height + 6, width, channels), F32),
                pltpu.VMEM((height + 6, wide, channels), F32),
                pltpu.VMEM((2, 3, wide, channels), F32),
                pltpu.VMEM((7, height + 6, width, channels), F32),
                pltpu.VMEM((height, width, channels), F32),
                pltpu.VMEM((cells, channels), F32),
                pltpu.VMEM((cells, 1), F32),
                pltpu.VMEM((cells, channels), BF16),
                pltpu.VMEM((cells, channels), BF16),
                pltpu.VMEM((cells, channels), F32),
                pltpu.VMEM((cells, channels), F32),
                pltpu.VMEM((4, cells, units // 4), F32),
                pltpu.VMEM((3, 49, channels), F32),
                pltpu.VMEM((4, subs, 2, block, 2 * channels), F32),
                pltpu.VMEM((4, subs, block, 2 * channels), F32),
                pltpu.VMEM((2, 3, subs, block, channels), F32),
                pltpu.VMEM((2, 3, subs, block, channels), F32),
                pltpu.VMEM((members, rows, 2 * channels), F32),
                pltpu.VMEM((members - 1, rows, 2 * channels), F32),
                pltpu.VMEM((2, TAP_HALF, channels), F32),
                pltpu.VMEM((TAP_HALF, channels), F32),
                pltpu.VMEM((4, TAP_HALF, channels), F32),
                pltpu.VMEM((members, TAP_HALF, channels), F32),
                pltpu.VMEM((2, TAP_HALF, channels), F32),
                dma((6,)), dma((2, 8)), dma((2, 8)), dma((4,)), dma((4,)), dma((2, 3)), dma((2, 3)),
                dma((members - 1,)), dma((members - 1,)), dma((5,)), dma((5,)),
                dma((members - 1,)), dma((members - 1,)),
            ],
            compiler_params=pltpu.CompilerParams(
                collective_id=0, has_side_effects=True, vmem_limit_bytes=60 * 1024 * 1024
            ),
            name="block",
        )(*args)
        out, gin, wgrad, gtaps, ggain = results
        return out, gin, wgrad, gtaps, ggain.reshape(channels)

    placed = (P("lat", "lon", None), P("lat", "lon", None), P(), P(), P(), P())
    return jax.shard_map(
        body,
        mesh=mesh,
        in_specs=placed,
        out_specs=(P("lat", "lon", None), P("lat", "lon", None), P(("lat", "lon"), None), P(), P()),
        check_vma=False,
    )
```

time: 55.7 us -> 52.3 us (0.939)
  the two profiles are of different devices: /device:TPU:19 before, /device:TPU:0 now
where the time goes in v2:
time: 52.3 us; the launch traced here: 52.1 us
  Pallas kernels  46.9 us (90%)
  local copies, waits for them, and re-layouts  4.52 us (9%)
  between operations  0.65 us (1%)
    pallas_call x1, Pallas kernels, body(): pl.pallas_call(functools.partial(kernel, n_lat, n_lon), out_shape=(jax.Sh...  46.9 us
    unnamed x13, local copies, waits for them, and re-layouts  4.52 us

profile of v2, /device:TPU:0, one launch (start us, length us, event | category | flops | bytes accessed | tf_op | source)
XLA Modules:
  0.0 52.1 jit_solution(16939282922674683677)
XLA Ops:
  0.6 46.9 %block.1 = (bf16[12,24,256]{2,1,0:T(8,128)(2,1)}, bf16[12,24,256]{2,1,0:T(8,128)(2,1)}, f32[32,512]{1,0:T(8,128)}, f32[49,256]{1,0:T(8,128)}, f32[1,256]{1,0:T(1,128)}) custom-call(f32[12,24,256]{2,1,0:T(8,128)} %state_h.1, bf16[12,24,256]{2,1,0:T(8,128)(2,1)} %cot_h.1, f32[49,256]{1,0:T(8,128)} %taps_h.1, f32[1,256]{1,0:T(1,128)} %bitcast.3, ...), custom_call_target="tpu_custom_call" | custom-call | tf_op jit(solution)/shard_map/block/pallas_call | solution.py:404
  47.5 0.0 copy-start
  47.5 1.6 %copy.16 = bf16[12,24,256]{2,1,0:T(8,128)(2,1)} copy(bf16[12,24,256]{2,1,0:T(8,128)(2,1)} %get-tuple-element.20) | data formatting | bytes 294912
  49.1 0.0 copy-done
  49.2 0.0 copy-start.1
  49.2 0.7 %copy.17 = bf16[12,24,256]{2,1,0:T(8,128)(2,1)} copy(bf16[12,24,256]{2,1,0:T(8,128)(2,1)S(1)} %copy-done) | data formatting | bytes 294912
  49.8 0.2 copy-done.1
  50.0 0.0 copy-start.2
  50.0 0.6 %copy.18 = f32[32,512]{1,0:T(8,128)} copy(f32[32,512]{1,0:T(8,128)S(1)} %copy-done.1) | data formatting | bytes 131072
  50.6 0.2 copy-done.2
  50.9 0.0 copy-start.3
  50.9 0.6 %copy.19 = f32[49,256]{1,0:T(8,128)} copy(f32[49,256]{1,0:T(8,128)S(1)} %copy-done.2) | data formatting | bytes 100352
  51.5 0.0 copy-done.3
  51.5 0.6 %copy.20 = f32[256]{0:T(256)} copy(f32[256]{0:T(256)S(1)} %bitcast.2) | data formatting | bytes 2048
Async XLA Ops:
  47.5 1.6 %copy-start = (bf16[12,24,256]{2,1,0:T(8,128)(2,1)S(1)}, bf16[12,24,256]{2,1,0:T(8,128)(2,1)}, u32[]{:S(2)}) copy-start(bf16[12,24,256]{2,1,0:T(8,128)(2,1)} %get-tuple-element.21) | copy-start | bytes 442372
  49.2 0.9 %copy-start.1 = (f32[32,512]{1,0:T(8,128)S(1)}, f32[32,512]{1,0:T(8,128)}, u32[]{:S(2)}) copy-start(f32[32,512]{1,0:T(8,128)} %get-tuple-element.22) | copy-start | bytes 196612
  50.0 0.8 %copy-start.2 = (f32[49,256]{1,0:T(8,128)S(1)}, f32[49,256]{1,0:T(8,128)}, u32[]{:S(2)}) copy-start(f32[49,256]{1,0:T(8,128)} %get-tuple-element.23) | copy-start | bytes 150532
  50.9 0.6 %copy-start.3 = (f32[1,256]{1,0:T(1,128)S(1)}, f32[1,256]{1,0:T(1,128)}, u32[]{:S(2)}) copy-start(f32[1,256]{1,0:T(1,128)} %get-tuple-element.14) | copy-start | bytes 3076

commit v3 on v2

--- a/solution.py
+++ b/solution.py
@@ -12,7 +12,6 @@
 F32 = jnp.float32
 BF16 = jnp.bfloat16
 SIDE = 8
-TAP_HALF = 32
 
 
 def dot(left, right, dims):
@@ -26,7 +25,7 @@
     state, cot, taps, gain, w_in, w_out,
     ext, rims, shifts, gext, grims, gshifts, conv, centred_s, istd_s, normed_s, cot_s,
     branch_s, gnorm_s, ghid_s, turned, local_w, core_w, pair_own, pair_got, group_own, group_got,
-    tap_mine, tap_far, tap_chip, tap_group, tap_done,
+    side_own, side_got, tap_mine, tap_far, tap_done,
     load_sem, halo_send, halo_recv, core_send, core_recv, pair_send, pair_recv,
     group_send, group_recv, tap_send, tap_recv, spread_send, spread_recv,
 ):
@@ -43,9 +42,11 @@
         load.start()
     height, width, channels = state.shape
     cells = height * width
+    pairs = height // 2
     units = w_in.shape[1]
     rows = units // (n_lat * n_lon)
     block = n_lon * rows
+    share_rows = -(-50 // (n_lat * n_lon))
     subs = n_lat // 8
     members = subs * n_lon
     chunk_rows = units // 4
@@ -81,21 +82,24 @@
         index = lax.rem(member + step, members)
         return index, (base + 2 * lax.div(index, n_lon), lax.rem(index, n_lon))
 
-    peers = []
-    for side in (-1, 0, 1):
-        peers.append((up_lat, wrap(lon + up_off + side)))
-        peers.append((down_lat, wrap(lon + down_off + side)))
-    peers.append((lat, wrap(lon - 1)))
-    peers.append((lat, wrap(lon + 1)))
-    peers.append(core_peer)
-    for code in range(1, 4):
-        peers.append(chip_peer(code))
-    for step in range(1, members):
-        peers.append(group_peer(step)[1])
+    devices = n_lat * n_lon
+    flat_id = lat * n_lon + lon
+
+    def device_at(step):
+        index = lax.rem(flat_id + step, devices)
+        return index, (lax.div(index, n_lon), lax.rem(index, n_lon))
+
     barrier = pltpu.get_barrier_semaphore()
-    for peer in peers:
-        pl.semaphore_signal(barrier, inc=1, device_id=peer, device_id_type=MESH)
-    pl.semaphore_wait(barrier, len(peers))
+
+    def greet(step, carry):
+        pl.semaphore_signal(
+            barrier, inc=1, device_id=device_at(step)[1], device_id_type=MESH
+        )
+        return carry
+
+    lax.fori_loop(1, devices, greet, 0)
+    loads[0].wait()
+    pl.semaphore_wait(barrier, devices - 1)
 
     def remote(source, target, send, recv, peer):
         return pltpu.make_async_remote_copy(
@@ -106,7 +110,7 @@
     spans = ((-1, 0, SIDE), (0, 0, width), (1, width - SIDE, SIDE))
     places = ((-1, SIDE + width), (0, SIDE), (1, 0))
 
-    def halo_copies(stage, source, whole, rim):
+    def halo_copies(stage, source, rim):
         copies = []
         for number, ((side, start, count), (_, place)) in enumerate(zip(spans, places)):
             for end, (peer_lat, off, slot) in enumerate(
@@ -122,22 +126,29 @@
                         (peer_lat, wrap(lon + off + side)),
                     )
                 )
-        copies.append(
-            remote(
-                source.at[:, pl.ds(0, SIDE)], whole.at[pl.ds(3, height), pl.ds(SIDE + width, SIDE)],
-                halo_send.at[stage, 6], halo_recv.at[stage, 6], (lat, wrap(lon - 1)),
+        for toward in range(2):
+            copies.append(
+                remote(
+                    side_own.at[stage, toward], side_got.at[stage, toward],
+                    halo_send.at[stage, 6 + toward], halo_recv.at[stage, 6 + toward],
+                    (lat, wrap(lon - 1 + 2 * toward)),
+                )
             )
-        )
-        copies.append(
-            remote(
-                source.at[:, pl.ds(width - SIDE, SIDE)], whole.at[pl.ds(3, height), pl.ds(0, SIDE)],
-                halo_send.at[stage, 7], halo_recv.at[stage, 7], (lat, wrap(lon + 1)),
-            )
-        )
         return copies
 
+    def start_halo(stage, source, local, rim):
+        copies = halo_copies(stage, source, rim)
+        for copy in copies[:6]:
+            copy.start()
+        for toward in range(2):
+            span = pl.ds(toward * (width - 4), 4)
+            for row in range(pairs):
+                side_own[stage, toward, row, pl.ds(0, 4), :] = local[row, span, :]
+                side_own[stage, toward, row, pl.ds(4, 4), :] = local[row + pairs, span, :]
+            copies[6 + toward].start()
+
     def finish_halo(stage, source, whole, rim, shifted):
-        copies = halo_copies(stage, source, whole, rim)
+        copies = halo_copies(stage, source, rim)
         for copy in copies:
             copy.wait_send()
         for copy in copies[6:]:
@@ -151,6 +162,11 @@
                     halo_recv.at[stage, 2 * number + slot],
                     (lat, wrap(lon + 1)),
                 ).wait_recv()
+        for toward, begin in ((0, SIDE + width), (1, SIDE - 4)):
+            span = pl.ds(begin, 4)
+            for row in range(pairs):
+                whole[3 + row, span, :] = side_got[stage, toward, row, pl.ds(0, 4), :]
+                whole[3 + row + pairs, span, :] = side_got[stage, toward, row, pl.ds(4, 4), :]
         for row in range(3):
             whole[row] = jnp.where(first, rim[0, 2 - row], rim[0, row])
             whole[height + 3 + row] = jnp.where(last, rim[1, 2 - row], rim[1, row])
@@ -162,10 +178,9 @@
 
         lax.fori_loop(0, height + 6, shift_row, 0)
 
-    for copy in halo_copies(0, state_h, ext, rims):
-        copy.start()
-
-    for load in loads:
+    start_halo(0, state_h, state, rims)
+
+    for load in loads[1:]:
         load.wait()
     ext[pl.ds(3, height), pl.ds(SIDE, width), :] = state[...]
     cot_s[...] = cot[...].astype(F32).reshape(cells, channels).astype(BF16)
@@ -255,12 +270,10 @@
             send_pair(1, 0, core_sum(0, 1))
         if turn == 2:
             send_pair(0, 1, core_sum(1, 0))
+        if turn == 3:
+            send_pair(1, 1, core_sum(2, 1))
             pair_copy(1, 0).wait()
             send_pair(1, 2, core_sum(1, 1) + pair_got[1, 0])
-        if turn == 3:
-            send_pair(1, 1, core_sum(2, 1))
-            pair_copy(0, 0).wait()
-            send_pair(0, 2, core_sum(2, 0) + pair_got[0, 0])
 
     gnorm = gnorm_s[...]
     centred = centred_s[...]
@@ -271,11 +284,59 @@
         - centred * jnp.mean(scaled * centred, axis=-1, keepdims=True)
     )
     conv[...] = grad_conv.reshape(height, width, channels)
-    for copy in halo_copies(1, conv, gext, grims):
-        copy.start()
+    start_halo(1, conv, conv, grims)
+    pair_copy(0, 0).wait()
+    send_pair(0, 2, core_sum(2, 0) + pair_got[0, 0])
     gext[pl.ds(3, height), pl.ds(SIDE, width), :] = conv[...]
-    tap_mine[1, pl.ds(TAP_HALF // 2, TAP_HALF // 2), :] = jnp.zeros((TAP_HALF // 2, channels), F32)
-    tap_mine[1, pl.ds(49 - TAP_HALF, 1), :] = jnp.sum(gnorm * centred, axis=0, keepdims=True)
+    def store_tap(index, value):
+        tap_mine[lax.div(index, share_rows), pl.ds(lax.rem(index, share_rows), 1), :] = value
+
+    def tap_row(index, carry):
+        row, col = lax.div(index, 7), lax.rem(index, 7)
+        total = jnp.zeros((width, channels), F32)
+        for line in range(height):
+            total = total + shifts[col, row + line] * conv[line]
+        store_tap(index, jnp.sum(total, axis=0, keepdims=True))
+        return carry
+
+    lax.fori_loop(0, 49, tap_row, 0)
+    store_tap(49, jnp.sum(gnorm * centred, axis=0, keepdims=True))
+
+    def clear_tap(index, carry):
+        store_tap(index, jnp.zeros((1, channels), F32))
+        return carry
+
+    lax.fori_loop(50, share_rows * devices, clear_tap, 0)
+
+    def scatter_copy(step):
+        index, peer = device_at(step)
+        return remote(
+            tap_mine.at[index], tap_far.at[step - 1],
+            tap_send.at[step - 1], tap_recv.at[step - 1], peer,
+        )
+
+    def gather_copy(step):
+        _, peer = device_at(step)
+        return remote(
+            tap_done.at[flat_id], tap_done.at[flat_id],
+            spread_send.at[step - 1], spread_recv.at[step - 1], peer,
+        )
+
+    def start_all(make):
+        def begin(step, carry):
+            make(step).start()
+            return carry
+
+        lax.fori_loop(1, devices, begin, 0)
+
+    def wait_all(make):
+        def finish(step, carry):
+            make(step).wait()
+            return carry
+
+        lax.fori_loop(1, devices, finish, 0)
+
+    start_all(scatter_copy)
 
     core_copy(3).wait()
     for stream in range(2):
@@ -298,39 +359,17 @@
     for step in range(1, members):
         group_copy(step).start()
 
-    def tap_row(index, carry):
-        row, col = lax.div(index, 7), lax.rem(index, 7)
-        total = jnp.zeros((width, channels), F32)
-        for line in range(height):
-            total = total + shifts[col, row + line] * conv[line]
-        tap_mine[lax.div(index, TAP_HALF), pl.ds(lax.rem(index, TAP_HALF), 1), :] = jnp.sum(
-            total, axis=0, keepdims=True
-        )
-        return carry
-
-    lax.fori_loop(0, 49, tap_row, 0)
-    tap_first = remote(
-        tap_mine.at[1 - core], tap_far, tap_send.at[0], tap_recv.at[0], core_peer
-    )
-    tap_first.start()
-
     out[...] = (
         state[...] + branch_s[...].reshape(height, width, channels)
     ).astype(BF16)
     finish_halo(1, conv, gext, grims, gshifts)
 
-    tap_first.wait()
-    quarter = 2 * high_y + high_x
-    tap_chip[quarter] = tap_mine[core] + tap_far[...]
-
-    def chip_copy(code):
-        return remote(
-            tap_chip.at[quarter], tap_chip.at[quarter],
-            tap_send.at[1 + code], tap_recv.at[1 + code], chip_peer(code),
-        )
-
-    for code in range(1, 4):
-        chip_copy(code).start()
+    scale = 1.0 / math.sqrt(cells * devices)
+    wait_all(scatter_copy)
+    total = tap_mine[flat_id]
+    total = total + jnp.sum(tap_far[...], axis=0)
+    tap_done[flat_id] = total * scale
+    start_all(gather_copy)
 
     def adjoint_row(index, carry):
         total = jnp.zeros((width, channels), F32)
@@ -342,25 +381,9 @@
         ext[index, pl.ds(0, width), :] = total
         return carry
 
-    lax.fori_loop(0, height // 2, adjoint_row, 0)
-
-    for code in range(1, 4):
-        chip_copy(code).wait()
-    tap_group[member] = (tap_chip[0] + tap_chip[1]) + (tap_chip[2] + tap_chip[3])
-
-    def spread_copy(step):
-        _, peer = group_peer(step)
-        return remote(
-            tap_group.at[member], tap_group.at[member],
-            spread_send.at[step - 1], spread_recv.at[step - 1], peer,
-        )
-
-    for step in range(1, members):
-        spread_copy(step).start()
-
-    lax.fori_loop(height // 2, height, adjoint_row, 0)
-
-    scale = 1.0 / math.sqrt(cells * n_lat * n_lon)
+    lax.fori_loop(0, height, adjoint_row, 0)
+    gin[...] = (cot[...].astype(F32) + ext[pl.ds(0, height), pl.ds(0, width), :]).astype(BF16)
+
     for step in range(1, members):
         group_copy(step).wait()
     total = group_own[member]
@@ -368,21 +391,10 @@
         total = total + group_got[step - 1]
     wgrad[...] = total * scale
 
-    for step in range(1, members):
-        spread_copy(step).wait()
-    total = tap_group[0]
-    for step in range(1, members):
-        total = total + tap_group[step]
-    tap_done[core] = total * scale
-    tap_last = remote(
-        tap_done.at[core], tap_done.at[core], tap_send.at[1], tap_recv.at[1], core_peer
-    )
-    tap_last.start()
-    gin[...] = (cot[...].astype(F32) + ext[pl.ds(0, height), pl.ds(0, width), :]).astype(BF16)
-    tap_last.wait()
-    gtaps[pl.ds(0, TAP_HALF), :] = tap_done[0]
-    gtaps[pl.ds(TAP_HALF, 49 - TAP_HALF), :] = tap_done[1, pl.ds(0, 49 - TAP_HALF), :]
-    ggain[...] = tap_done[1, pl.ds(49 - TAP_HALF, 1), :]
+    wait_all(gather_copy)
+    for index in range(49):
+        gtaps[pl.ds(index, 1), :] = tap_done[index // share_rows, pl.ds(index % share_rows, 1), :]
+    ggain[...] = tap_done[49 // share_rows, pl.ds(49 % share_rows, 1), :]
 
 
 def solution(mesh):
@@ -396,6 +408,8 @@
         block = n_lon * rows
         subs = n_lat // 8
         members = subs * n_lon
+        devices = n_lat * n_lon
+        share_rows = -(-50 // devices)
         wide = width + 2 * SIDE
         vmem = pl.BlockSpec(memory_space=pltpu.VMEM)
         hbm = pl.BlockSpec(memory_space=pl.ANY)
@@ -434,14 +448,14 @@
                 pltpu.VMEM((2, 3, subs, block, channels), F32),
                 pltpu.VMEM((members, rows, 2 * channels), F32),
                 pltpu.VMEM((members - 1, rows, 2 * channels), F32),
-                pltpu.VMEM((2, TAP_HALF, channels), F32),
-                pltpu.VMEM((TAP_HALF, channels), F32),
-                pltpu.VMEM((4, TAP_HALF, channels), F32),
-                pltpu.VMEM((members, TAP_HALF, channels), F32),
-                pltpu.VMEM((2, TAP_HALF, channels), F32),
+                pltpu.VMEM((2, 2, height // 2, 8, channels), F32),
+                pltpu.VMEM((2, 2, height // 2, 8, channels), F32),
+                pltpu.VMEM((devices, share_rows, channels), F32),
+                pltpu.VMEM((devices - 1, share_rows, channels), F32),
+                pltpu.VMEM((devices, share_rows, channels), F32),
                 dma((6,)), dma((2, 8)), dma((2, 8)), dma((4,)), dma((4,)), dma((2, 3)), dma((2, 3)),
-                dma((members - 1,)), dma((members - 1,)), dma((5,)), dma((5,)),
-                dma((members - 1,)), dma((members - 1,)),
+                dma((members - 1,)), dma((members - 1,)), dma((devices - 1,)), dma((devices - 1,)),
+                dma((devices - 1,)), dma((devices - 1,)),
             ],
             compiler_params=pltpu.CompilerParams(
                 collective_id=0, has_side_effects=True, vmem_limit_bytes=60 * 1024 * 1024

time: 52.3 us -> 49.1 us (0.939)
  Pallas kernels: 46.9 us -> 43.7 us
    pallas_call x1, Pallas kernels: 46.9 us -> 43.7 us  [body(): pl.pallas_call(functools.partial(kernel, n_lat, n_lon), out_shape=(jax.Sh...]
where the time goes in v3:
time: 49.1 us; the launch traced here: 48.8 us
  Pallas kernels  43.7 us (89%)
  local copies, waits for them, and re-layouts  4.52 us (9%)
  between operations  0.65 us (1%)
    pallas_call x1, Pallas kernels, body(): pl.pallas_call(functools.partial(kernel, n_lat, n_lon), out_shape=(jax.Sh...  43.7 us
    unnamed x13, local copies, waits for them, and re-layouts  4.52 us

profile of v3, /device:TPU:0, one launch (start us, length us, event | category | flops | bytes accessed | tf_op | source)
XLA Modules:
  0.0 48.8 jit_solution(12925400376519145751)
XLA Ops:
  0.6 43.7 %block.1 = (bf16[12,24,256]{2,1,0:T(8,128)(2,1)}, bf16[12,24,256]{2,1,0:T(8,128)(2,1)}, f32[32,512]{1,0:T(8,128)}, f32[49,256]{1,0:T(8,128)}, f32[1,256]{1,0:T(1,128)}) custom-call(f32[12,24,256]{2,1,0:T(8,128)} %state_h.1, bf16[12,24,256]{2,1,0:T(8,128)(2,1)} %cot_h.1, f32[49,256]{1,0:T(8,128)} %taps_h.1, f32[1,256]{1,0:T(1,128)} %bitcast.3, ...), custom_call_target="tpu_custom_call" | custom-call | tf_op jit(solution)/shard_map/block/pallas_call | solution.py:418
  44.3 0.0 copy-start
  44.3 1.6 %copy.16 = bf16[12,24,256]{2,1,0:T(8,128)(2,1)} copy(bf16[12,24,256]{2,1,0:T(8,128)(2,1)} %get-tuple-element.20) | data formatting | bytes 294912
  45.9 0.0 copy-done
  45.9 0.0 copy-start.1
  45.9 0.7 %copy.17 = bf16[12,24,256]{2,1,0:T(8,128)(2,1)} copy(bf16[12,24,256]{2,1,0:T(8,128)(2,1)S(1)} %copy-done) | data formatting | bytes 294912
  46.6 0.2 copy-done.1
  46.8 0.0 copy-start.2
  46.8 0.6 %copy.18 = f32[32,512]{1,0:T(8,128)} copy(f32[32,512]{1,0:T(8,128)S(1)} %copy-done.1) | data formatting | bytes 131072
  47.4 0.2 copy-done.2
  47.6 0.0 copy-start.3
  47.6 0.6 %copy.19 = f32[49,256]{1,0:T(8,128)} copy(f32[49,256]{1,0:T(8,128)S(1)} %copy-done.2) | data formatting | bytes 100352
  48.3 0.0 copy-done.3
  48.3 0.6 %copy.20 = f32[256]{0:T(256)} copy(f32[256]{0:T(256)S(1)} %bitcast.2) | data formatting | bytes 2048
Async XLA Ops:
  44.3 1.6 %copy-start = (bf16[12,24,256]{2,1,0:T(8,128)(2,1)S(1)}, bf16[12,24,256]{2,1,0:T(8,128)(2,1)}, u32[]{:S(2)}) copy-start(bf16[12,24,256]{2,1,0:T(8,128)(2,1)} %get-tuple-element.21) | copy-start | bytes 442372
  45.9 0.9 %copy-start.1 = (f32[32,512]{1,0:T(8,128)S(1)}, f32[32,512]{1,0:T(8,128)}, u32[]{:S(2)}) copy-start(f32[32,512]{1,0:T(8,128)} %get-tuple-element.22) | copy-start | bytes 196612
  46.8 0.8 %copy-start.2 = (f32[49,256]{1,0:T(8,128)S(1)}, f32[49,256]{1,0:T(8,128)}, u32[]{:S(2)}) copy-start(f32[49,256]{1,0:T(8,128)} %get-tuple-element.23) | copy-start | bytes 150532
  47.6 0.6 %copy-start.3 = (f32[1,256]{1,0:T(1,128)S(1)}, f32[1,256]{1,0:T(1,128)}, u32[]{:S(2)}) copy-start(f32[1,256]{1,0:T(1,128)} %get-tuple-element.14) | copy-start | bytes 3076

commit v4 on v3

--- a/solution.py
+++ b/solution.py
@@ -12,6 +12,7 @@
 F32 = jnp.float32
 BF16 = jnp.bfloat16
 SIDE = 8
+GROUP = 4
 
 
 def dot(left, right, dims):
@@ -24,7 +25,7 @@
     out, gin, wgrad, gtaps, ggain,
     state, cot, taps, gain, w_in, w_out,
     ext, rims, shifts, gext, grims, gshifts, conv, centred_s, istd_s, normed_s, cot_s,
-    branch_s, gnorm_s, ghid_s, turned, local_w, core_w, pair_own, pair_got, group_own, group_got,
+    branch_s, gnorm_s, ghid_s, spread, turned, local_w, core_w, pair_own, pair_got, group_own, group_got,
     side_own, side_got, tap_mine, tap_far, tap_done,
     load_sem, halo_send, halo_recv, core_send, core_recv, pair_send, pair_recv,
     group_send, group_recv, tap_send, tap_recv, spread_send, spread_recv,
@@ -190,24 +191,40 @@
         )
     for row in range(7):
         for col in range(7):
-            plain = taps[pl.ds(48 - 7 * row - col, 1), :]
-            mirrored = taps[pl.ds(7 * row + 6 - col, 1), :]
-            spot = pl.ds(7 * row + col, 1)
-            turned[0, spot, :] = jnp.where(first, mirrored, plain)
-            turned[1, spot, :] = plain
-            turned[2, spot, :] = jnp.where(last, mirrored, plain)
+            wide_shape = (8, channels)
+            forward = jnp.broadcast_to(taps[pl.ds(7 * row + col, 1), :], wide_shape)
+            plain = jnp.broadcast_to(taps[pl.ds(48 - 7 * row - col, 1), :], wide_shape)
+            mirrored = jnp.broadcast_to(taps[pl.ds(7 * row + 6 - col, 1), :], wide_shape)
+            spot = 7 * row + col
+            spread[spot] = forward
+            turned[0, spot] = jnp.where(first, mirrored, plain)
+            turned[1, spot] = plain
+            turned[2, spot] = jnp.where(last, mirrored, plain)
 
     finish_halo(0, state_h, ext, rims, shifts)
 
-    def conv_row(index, carry):
-        total = jnp.zeros((width, channels), F32)
-        for row in range(7):
-            for col in range(7):
-                total = total + shifts[col, index + row] * taps[pl.ds(7 * row + col, 1), :]
-        conv[index] = total
-        return carry
-
-    lax.fori_loop(0, height, conv_row, 0)
+    def filtered(source, weight_of, store):
+        def step(group, carry):
+            begin = group * GROUP
+            totals = [jnp.zeros((width // 8, 8, channels), F32) for _ in range(GROUP)]
+            for line in range(GROUP + 6):
+                for col in range(7):
+                    cells_in = source[col, begin + line].reshape(width // 8, 8, channels)
+                    for out_row in range(GROUP):
+                        if 0 <= line - out_row < 7:
+                            totals[out_row] = totals[out_row] + cells_in * weight_of(
+                                begin + line, line - out_row, col
+                            )
+            for out_row in range(GROUP):
+                store(begin + out_row, totals[out_row].reshape(width, channels))
+            return carry
+
+        lax.fori_loop(0, height // GROUP, step, 0)
+
+    def store_conv(row, value):
+        conv[row] = value
+
+    filtered(shifts, lambda line, row, col: spread[7 * row + col], store_conv)
 
     flat = conv[...].reshape(cells, channels)
     raw = flat - jnp.mean(flat, axis=-1, keepdims=True)
@@ -291,15 +308,19 @@
     def store_tap(index, value):
         tap_mine[lax.div(index, share_rows), pl.ds(lax.rem(index, share_rows), 1), :] = value
 
-    def tap_row(index, carry):
-        row, col = lax.div(index, 7), lax.rem(index, 7)
-        total = jnp.zeros((width, channels), F32)
+    def tap_column(col, carry):
+        totals = [jnp.zeros((8, channels), F32) for _ in range(7)]
         for line in range(height):
-            total = total + shifts[col, row + line] * conv[line]
-        store_tap(index, jnp.sum(total, axis=0, keepdims=True))
+            grads = conv[line].reshape(width // 8, 8, channels)
+            for row in range(7):
+                terms = shifts[col, row + line].reshape(width // 8, 8, channels) * grads
+                for part in range(width // 8):
+                    totals[row] = totals[row] + terms[part]
+        for row in range(7):
+            store_tap(7 * row + col, jnp.sum(totals[row], axis=0, keepdims=True))
         return carry
 
-    lax.fori_loop(0, 49, tap_row, 0)
+    lax.fori_loop(0, 7, tap_column, 0)
     store_tap(49, jnp.sum(gnorm * centred, axis=0, keepdims=True))
 
     def clear_tap(index, carry):
@@ -371,17 +392,14 @@
     tap_done[flat_id] = total * scale
     start_all(gather_copy)
 
-    def adjoint_row(index, carry):
-        total = jnp.zeros((width, channels), F32)
-        for row in range(7):
-            line = index + row
-            kind = jnp.where(line < 3, 0, jnp.where(line >= height + 3, 2, 1))
-            for col in range(7):
-                total = total + gshifts[col, line] * turned[kind, pl.ds(7 * row + col, 1), :]
-        ext[index, pl.ds(0, width), :] = total
-        return carry
-
-    lax.fori_loop(0, height, adjoint_row, 0)
+    def turned_at(line, row, col):
+        kind = jnp.where(line < 3, 0, jnp.where(line >= height + 3, 2, 1))
+        return turned[kind, 7 * row + col]
+
+    def store_adjoint(row, value):
+        ext[row, pl.ds(0, width), :] = value
+
+    filtered(gshifts, turned_at, store_adjoint)
     gin[...] = (cot[...].astype(F32) + ext[pl.ds(0, height), pl.ds(0, width), :]).astype(BF16)
 
     for step in range(1, members):
@@ -412,7 +430,7 @@
         share_rows = -(-50 // devices)
         wide = width + 2 * SIDE
         vmem = pl.BlockSpec(memory_space=pltpu.VMEM)
-        hbm = pl.BlockSpec(memory_space=pl.ANY)
+        hbm = pl.BlockSpec(memory_space=pltpu.HBM)
         dma = pltpu.SemaphoreType.DMA
         args = (state, cot, taps, gain.reshape(1, channels), w_in, w_out)
         results = pl.pallas_call(
@@ -441,7 +459,8 @@
                 pltpu.VMEM((cells, channels), F32),
                 pltpu.VMEM((cells, channels), F32),
                 pltpu.VMEM((4, cells, units // 4), F32),
-                pltpu.VMEM((3, 49, channels), F32),
+                pltpu.VMEM((49, 8, channels), F32),
+                pltpu.VMEM((3, 49, 8, channels), F32),
                 pltpu.VMEM((4, subs, 2, block, 2 * channels), F32),
                 pltpu.VMEM((4, subs, block, 2 * channels), F32),
                 pltpu.VMEM((2, 3, subs, block, channels), F32),
@@ -458,7 +477,7 @@
                 dma((devices - 1,)), dma((devices - 1,)),
             ],
             compiler_params=pltpu.CompilerParams(
-                collective_id=0, has_side_effects=True, vmem_limit_bytes=60 * 1024 * 1024
+                collective_id=0, has_side_effects=True, vmem_limit_bytes=40 * 1024 * 1024
             ),
             name="block",
         )(*args)

time: 49.1 us -> 51.3 us (1.045)
  local copies, waits for them, and re-layouts: 4.52 us -> 8.58 us
  Pallas kernels: 43.7 us -> 41.8 us
    unnamed x13 -> x17, local copies, waits for them, and re-layouts: 4.52 us -> 8.58 us
    pallas_call x1, Pallas kernels: 43.7 us -> 41.8 us  [body(): pl.pallas_call(functools.partial(kernel, n_lat, n_lon), out_shape=(jax.Sh...]
where the time goes in v4:
time: 51.3 us; the launch traced here: 51 us
  Pallas kernels  41.8 us (81%)
  local copies, waits for them, and re-layouts  8.58 us (17%)
  between operations  0.66 us (1%)
    pallas_call x1, Pallas kernels, body(): pl.pallas_call(functools.partial(kernel, n_lat, n_lon), out_shape=(jax.Sh...  41.8 us
    unnamed x17, local copies, waits for them, and re-layouts  8.58 us

profile of v4, /device:TPU:0, one launch (start us, length us, event | category | flops | bytes accessed | tf_op | source)
XLA Modules:
  0.0 51.0 jit_solution(10983585999477115281)
XLA Ops:
  0.6 0.0 copy-start.5
  0.6 0.7 %copy-done.5 = f32[256]{0:T(256)S(1)} copy-done((f32[256]{0:T(256)S(1)}, f32[256]{0:T(256)}, u32[]{:S(2)}) %copy-start.5) | copy-done | bytes 1048
  1.3 0.0 copy-start
  1.3 1.0 %copy-done = bf16[256,1024]{1,0:T(8,128)(2,1)S(1)} copy-done((bf16[256,1024]{1,0:T(8,128)(2,1)S(1)}, bf16[256,1024]{1,0:T(8,128)(2,1)}, u32[]{:S(2)}) %copy-start) | copy-done | bytes 524312
  2.4 0.0 copy-start.1
  2.4 1.0 %copy-done.1 = bf16[1024,256]{1,0:T(8,128)(2,1)S(1)} copy-done((bf16[1024,256]{1,0:T(8,128)(2,1)S(1)}, bf16[1024,256]{1,0:T(8,128)(2,1)}, u32[]{:S(2)}) %copy-start.1) | copy-done | bytes 524312
  3.4 0.0 copy-start.2
  3.4 1.0 %copy-done.2 = f32[12,24,256]{2,1,0:T(8,128)S(1)} copy-done((f32[12,24,256]{2,1,0:T(8,128)S(1)}, f32[12,24,256]{2,1,0:T(8,128)}, u32[]{:S(2)}) %copy-start.2) | copy-done | bytes 294936
  4.4 0.0 copy-start.3
  4.4 0.9 %copy-done.3 = bf16[12,24,256]{2,1,0:T(8,128)(2,1)S(1)} copy-done((bf16[12,24,256]{2,1,0:T(8,128)(2,1)S(1)}, bf16[12,24,256]{2,1,0:T(8,128)(2,1)}, u32[]{:S(2)}) %copy-start.3) | copy-done | bytes 147480
  5.3 0.0 copy-start.4
  5.3 0.8 %copy-done.4 = f32[49,256]{1,0:T(8,128)S(1)} copy-done((f32[49,256]{1,0:T(8,128)S(1)}, f32[49,256]{1,0:T(8,128)}, u32[]{:S(2)}) %copy-start.4) | copy-done | bytes 50200
  6.1 41.8 %block.1 = (bf16[12,24,256]{2,1,0:T(8,128)(2,1)S(1)}, bf16[12,24,256]{2,1,0:T(8,128)(2,1)S(1)}, f32[32,512]{1,0:T(8,128)S(1)}, f32[49,256]{1,0:T(8,128)S(1)}, f32[1,256]{1,0:T(1,128)S(1)}) custom-call(f32[12,24,256]{2,1,0:T(8,128)S(1)} %copy-done.2, bf16[12,24,256]{2,1,0:T(8,128)(2,1)S(1)} %copy-done.3, f32[49,256]{1,0:T(8,128)S(1)} %copy-done.4, ...), custom_call_target="tpu_custom_call" | custom-call | tf_op jit(solution)/shard_map/block/pallas_call | solution.py:436
  47.9 0.7 %copy.16 = bf16[12,24,256]{2,1,0:T(8,128)(2,1)} copy(bf16[12,24,256]{2,1,0:T(8,128)(2,1)S(1)} %get-tuple-element.20) | data formatting | bytes 294912
  48.5 0.7 %copy.17 = bf16[12,24,256]{2,1,0:T(8,128)(2,1)} copy(bf16[12,24,256]{2,1,0:T(8,128)(2,1)S(1)} %get-tuple-element.21) | data formatting | bytes 294912
  49.2 0.6 %copy.18 = f32[32,512]{1,0:T(8,128)} copy(f32[32,512]{1,0:T(8,128)S(1)} %get-tuple-element.22) | data formatting | bytes 131072
  49.8 0.6 %copy.19 = f32[49,256]{1,0:T(8,128)} copy(f32[49,256]{1,0:T(8,128)S(1)} %get-tuple-element.23) | data formatting | bytes 100352
  50.4 0.6 %copy.20 = f32[256]{0:T(256)} copy(f32[256]{0:T(256)S(1)} %bitcast.2) | data formatting | bytes 2048
Async XLA Ops:
  0.6 0.7 %copy-start.5 = (f32[256]{0:T(256)S(1)}, f32[256]{0:T(256)}, u32[]{:S(2)}) copy-start(f32[256]{0:T(256)} %param.9) | copy-start | bytes 3076
  1.3 1.0 %copy-start = (bf16[256,1024]{1,0:T(8,128)(2,1)S(1)}, bf16[256,1024]{1,0:T(8,128)(2,1)}, u32[]{:S(2)}) copy-start(bf16[256,1024]{1,0:T(8,128)(2,1)} %w_in_h.1) | copy-start | bytes 1572868
  2.4 1.0 %copy-start.1 = (bf16[1024,256]{1,0:T(8,128)(2,1)S(1)}, bf16[1024,256]{1,0:T(8,128)(2,1)}, u32[]{:S(2)}) copy-start(bf16[1024,256]{1,0:T(8,128)(2,1)} %w_out_h.1) | copy-start | bytes 1572868
  3.4 1.0 %copy-start.2 = (f32[12,24,256]{2,1,0:T(8,128)S(1)}, f32[12,24,256]{2,1,0:T(8,128)}, u32[]{:S(2)}) copy-start(f32[12,24,256]{2,1,0:T(8,128)} %state_h.1) | copy-start | bytes 884740
  4.4 0.9 %copy-start.3 = (bf16[12,24,256]{2,1,0:T(8,128)(2,1)S(1)}, bf16[12,24,256]{2,1,0:T(8,128)(2,1)}, u32[]{:S(2)}) copy-start(bf16[12,24,256]{2,1,0:T(8,128)(2,1)} %cot_h.1) | copy-start | bytes 442372
  5.3 0.8 %copy-start.4 = (f32[49,256]{1,0:T(8,128)S(1)}, f32[49,256]{1,0:T(8,128)}, u32[]{:S(2)}) copy-start(f32[49,256]{1,0:T(8,128)} %taps_h.1) | copy-start | bytes 150532
